TPU v7x, 32 devices: a whole 2x2x4 slice. The times are simulated.
32 devices in a mesh: groups: 2 (over y), freq: 16 (over z, x, core).
Axes of the slice: x: 2, y: 2, z: 4, core: 2. Of those that a mesh axis runs over, the one named last changes fastest.
Arguments:
- signal: float32 [1024, 8, 4096], P('freq', None, 'groups'), parts along dimension 2, may hold values from -6 to 6
- offsets: int32 [8], replicated, may hold values from 0 to 4095
- pairing: int32 [4096], P('groups'), parts along dimension 0, may hold values from 0 to 2047, each once
- modes_kept: int32 [512], replicated, may hold values from 1 to 4, as said below
Outputs:
- energy: float32 [512, 8], P('freq', 'groups'), parts along dimension 1
- modes: float32 [512, 4, 2, 2, 2048], P(None, None, None, None, ('groups', 'freq')), parts along dimension 4
There are 2 independent parts, one for each index of `groups`. A program takes and returns all parts, laid end to end along the dimension named above; an argument that names none is the same for every part. Nothing has to cross between parts.
Inputs may be any that keep to these rules, and one draw needn't show every extreme that they name: `modes_kept`: every value from 1 to 4 occurs. `pairing`: a permutation of the 2048 points.
All inputs are finite; a program needn't handle non-finite values.
Results may differ from a plain program's by a relative error of at most 0.0001.
Values sent between devices are 32-bit elements; how exact they have to be, the bound alone decides.
No kernel may reach another device: no remote copies, remote signals or barrier semaphores. Data moves between devices by JAX's collectives and lax.ppermute only.
A program may use at most 128 MiB of HBM per device.

v0:
```python
import math

import jax
import jax.numpy as jnp
from jax import lax
from jax.sharding import PartitionSpec as P

NF1 = 128
P_SIZE = 2048
M = 4
ITERS = 3


precise = lax.Precision.HIGHEST


def twiddles(rows_total, cols_total, period):
    left_side = jnp.arange(rows_total, dtype=jnp.int32)[:, None]
    right_side = jnp.arange(cols_total, dtype=jnp.int32)[None, :]
    phase = (left_side * right_side % period).astype(jnp.float32) * (2.0 * math.pi / period)
    return (jnp.cos(phase), jnp.sin(phase))


def hann_window(frames):
    steps = jnp.arange(frames, dtype=jnp.int32).astype(jnp.float32)
    shape = 0.5 - 0.5 * jnp.cos(2.0 * math.pi / frames * steps)
    return shape / jnp.sqrt(jnp.sum(shape * shape))


def rotate_lanes(values):
    half = values.shape[-1] // 2
    return jnp.concatenate([values[..., half:], -values[..., :half]], axis=-1)


def swap_lanes(values):
    half = values.shape[-1] // 2
    return jnp.concatenate([values[..., half:], values[..., :half]], axis=-1)


def four_step(flat):
    frames, lanes = flat.shape
    outer = NF1
    inner = frames // outer
    window = hann_window(frames)[:, None]
    shaped = (flat * window).reshape(outer, inner, lanes)
    cos_outer, sin_outer = twiddles(outer, outer, outer)
    section = jnp.einsum("ij,jsl->isl", cos_outer, shaped, precision=precise) + jnp.einsum(
        "ij,jsl->isl", sin_outer, rotate_lanes(shaped), precision=precise
    )
    cos_twist, sin_twist = twiddles(outer, inner, frames)
    section = section * cos_twist[:, :, None] + rotate_lanes(section) * sin_twist[:, :, None]
    cos_inner, sin_inner = twiddles(inner, inner, inner)
    result = jnp.einsum("js,ksl->jkl", cos_inner, section, precision=precise) + jnp.einsum(
        "js,ksl->jkl", sin_inner, rotate_lanes(section), precision=precise
    )
    return result.reshape(frames, lanes)


def unpack_pairs(spectrum, offsets, blocks):
    frames, lanes = spectrum.shape
    half_bins = frames // 2
    half_lanes = lanes // 2
    pair_count = half_lanes // blocks
    mirror = jnp.roll(jnp.flip(spectrum, 0), 1, 0)[:half_bins]
    direct = spectrum[:half_bins]
    signs = jnp.concatenate(
        [jnp.ones((half_lanes,), jnp.float32), -jnp.ones((half_lanes,), jnp.float32)]
    )
    first = 0.5 * (direct + mirror * signs[None, :])
    second = 0.5 * (rotate_lanes(direct) + swap_lanes(mirror))
    bins = jnp.arange(half_bins, dtype=jnp.int32)
    lane_offsets = jnp.tile(jnp.repeat(offsets, pair_count), 2)
    phase = (bins[:, None] * lane_offsets[None, :] % frames).astype(jnp.float32) * (
        2.0 * math.pi / frames
    )
    cos_part = jnp.cos(phase)
    sin_part = jnp.sin(phase)
    first = first * cos_part + rotate_lanes(first) * sin_part
    second = second * cos_part + rotate_lanes(second) * sin_part
    return jnp.stack([first, second], axis=1)


def split_view(spectra, blocks):
    bins = spectra.shape[0]
    shaped = spectra.reshape(bins, 2, 2, blocks, -1)
    return (shaped[:, :, 0], shaped[:, :, 1])


def gram_of(spectra, points, blocks):
    u_re, u_im = split_view(spectra, blocks)
    g_re = jnp.einsum("kwbp,kwcp->kbc", u_re, u_re, precision=precise) + jnp.einsum(
        "kwbp,kwcp->kbc", u_im, u_im, precision=precise
    )
    g_im = jnp.einsum("kwbp,kwcp->kbc", u_re, u_im, precision=precise) - jnp.einsum(
        "kwbp,kwcp->kbc", u_im, u_re, precision=precise
    )
    return jnp.stack([g_re, g_im], axis=1) / points


def complex_product(a_re, a_im, b_re, b_im):
    out_re = jnp.einsum("kij,kjm->kim", a_re, b_re, precision=precise) - jnp.einsum(
        "kij,kjm->kim", a_im, b_im, precision=precise
    )
    out_im = jnp.einsum("kij,kjm->kim", a_re, b_im, precision=precise) + jnp.einsum(
        "kij,kjm->kim", a_im, b_re, precision=precise
    )
    return (out_re, out_im)


def leading_basis(gram):
    g_re = gram[:, 0]
    g_im = gram[:, 1]
    number = g_re.shape[0]
    blocks = g_re.shape[1]
    q_re = jnp.broadcast_to(jnp.eye(blocks, M, dtype=jnp.float32), (number, blocks, M))
    q_im = jnp.zeros_like(q_re)
    for sweep_index in range(ITERS):
        y_re, y_im = complex_product(g_re, g_im, q_re, q_im)
        done_re = []
        done_im = []
        for column in range(M):
            v_re = y_re[:, :, column]
            v_im = y_im[:, :, column]
            for earlier in range(column):
                p_re = done_re[earlier]
                p_im = done_im[earlier]
                proj_re = jnp.sum(p_re * v_re + p_im * v_im, axis=1, keepdims=True)
                proj_im = jnp.sum(p_re * v_im - p_im * v_re, axis=1, keepdims=True)
                v_re = v_re - (proj_re * p_re - proj_im * p_im)
                v_im = v_im - (proj_re * p_im + proj_im * p_re)
            length = jnp.sqrt(jnp.sum(v_re * v_re + v_im * v_im, axis=1, keepdims=True))
            done_re.append(v_re / length)
            done_im.append(v_im / length)
        q_re = jnp.stack(done_re, axis=2)
        q_im = jnp.stack(done_im, axis=2)
    gq_re, gq_im = complex_product(g_re, g_im, q_re, q_im)
    energy = jnp.sum(q_re * gq_re + q_im * gq_im, axis=1)
    return (jnp.stack([q_re, q_im], axis=1), energy)


def project(spectra, basis, energy, kept, blocks):
    u_re, u_im = split_view(spectra, blocks)
    q_re = basis[:, 0]
    q_im = basis[:, 1]
    m_re = jnp.einsum("kwbp,kbm->kmwp", u_re, q_re, precision=precise) - jnp.einsum(
        "kwbp,kbm->kmwp", u_im, q_im, precision=precise
    )
    m_im = jnp.einsum("kwbp,kbm->kmwp", u_re, q_im, precision=precise) + jnp.einsum(
        "kwbp,kbm->kmwp", u_im, q_re, precision=precise
    )
    live = (jnp.arange(M, dtype=jnp.int32)[None, :] < kept[:, None]).astype(jnp.float32)
    factor = (live / jnp.sqrt(energy))[:, :, None, None]
    return jnp.stack([m_re * factor, m_im * factor], axis=2)


def local(signal, offsets, pairing, modes_kept):
    blocks = signal.shape[1]
    first_part = jnp.take(signal, pairing[0::2], axis=2)
    second_part = jnp.take(signal, pairing[1::2], axis=2)
    packed = jnp.stack([first_part, second_part], axis=1)
    frames_all = lax.all_to_all(packed, "freq", split_axis=3, concat_axis=0, tiled=True)
    flat = frames_all.reshape(frames_all.shape[0], -1)
    spectrum = four_step(flat)
    spectra = unpack_pairs(spectrum, offsets, blocks)
    local_bins = spectra.shape[0] // lax.axis_size("freq")
    shaped = spectra.reshape(spectra.shape[0], 2, 2, blocks, -1)
    owned = lax.all_to_all(shaped, "freq", split_axis=0, concat_axis=4, tiled=True)
    owned = owned.reshape(owned.shape[0], 2, -1)
    gram = gram_of(owned, P_SIZE, blocks)
    basis, energy = leading_basis(gram)
    kept = lax.dynamic_slice_in_dim(modes_kept, lax.axis_index("freq") * local_bins, local_bins)
    local_modes = project(owned, basis, energy, kept, blocks)
    modes = lax.all_to_all(local_modes, "freq", split_axis=4, concat_axis=0, tiled=True)
    return (energy, modes)


def solution(mesh):
    placed = (P("freq", None, "groups"), P(), P("groups"), P())
    return jax.shard_map(
        local,
        mesh=mesh,
        in_specs=placed,
        out_specs=(P("freq", "groups"), P(None, None, None, None, ("groups", "freq"))),
        check_vma=False,
    )
```

profile of v0, /device:TPU:0, one launch (start us, length us, event | category | flops | bytes accessed | tf_op | source)
XLA Modules:
  0.0 604.9 jit_solution(13675092589313280987)
XLA Ops:
  2.5 7.5 %copy.625 = f32[64,8,2048]{0,1,2:T(8,128)} copy(f32[64,8,2048]{2,1,0:T(8,128)} %param.6) | data formatting | bytes 8388608 | tf_op args[0]
  10.0 11.6 %gather_fusion = f32[1024,64,8]{1,2,0:T(8,128)} fusion(f32[64,8,2048]{0,1,2:T(8,128)} %copy.625, s32[1024]{0:T(1024)S(1)} %fusion.150), kind=kCustom, calls=%fused_computation.clone | custom fusion | bytes 4198400 | tf_op jit(solution)/shard_map/jit(_take)/gather | solution.py:158
  21.5 11.6 %gather_fusion.1 = f32[1024,64,8]{1,2,0:T(8,128)} fusion(f32[64,8,2048]{0,1,2:T(8,128)} %copy.625, s32[1024]{0:T(1024)S(1)} %fusion.151), kind=kCustom, calls=%fused_computation.1.clone | custom fusion | bytes 4198400 | tf_op jit(solution)/shard_map/jit(_take)/gather | solution.py:159
  42.9 13.3 %reshape.1843 = f32[16,1,65536]{2,1,0:T(1,128)} reshape(f32[1024,2,8,64]{3,2,1,0:T(8,128)} %copy_bitcast_fusion) | data formatting | bytes 8388608
  56.2 7.5 %all-to-all-start = ((f32[16,1,65536]{2,1,0:T(1,128)}), f32[16,1,65536]{2,1,0:T(1,128)}, u32[]{:S(2)}, u32[]{:S(2)}) async-start(f32[16,1,65536]{2,1,0:T(1,128)} %reshape.1843), calls=%async_computation | async-start | bytes 8388608 | tf_op jit(solution)/shard_map/all_to_all | solution.py:161
  65.3 76.1 %all-to-all-done = f32[16,1,65536]{2,1,0:T(1,128)} async-done(((f32[16,1,65536]{2,1,0:T(1,128)}), f32[16,1,65536]{2,1,0:T(1,128)}, u32[]{:S(2)}, u32[]{:S(2)}) %all-to-all-start) | async-done | bytes 4194336 | tf_op jit(solution)/shard_map/all_to_all | solution.py:161
  141.9 13.6 %reduce = f32[16,65536]{1,0:T(8,128)} reduce(f32[16,1,65536]{2,1,0:T(1,128)} %all-to-all-done, f32[]{:T(128)} %broadcast.1485), dimensions={1}, to_apply=%all_to_all.37.reduce_sub_computation | reduce | bytes 8388612 | tf_op jit(solution)/shard_map/all_to_all | solution.py:161
  155.5 6.9 %reshape.1844 = f32[1024,2,8,64]{3,2,1,0:T(8,128)} reshape(f32[16,65536]{1,0:T(8,128)} %reduce) | data formatting | bytes 8388608
  162.4 10.4 %copy.628 = f32[64,2,8,16,64]{4,2,1,0,3:T(8,128)} copy(f32[64,2,8,16,64]{0,2,1,4,3:T(8,128)} %bitcast.590) | data formatting | bytes 8388608 | tf_op jit(solution)/shard_map/all_to_all | solution.py:161
  172.8 8.1 %reshape.1807 = f32[128,8,1024]{2,1,0:T(8,128)} reshape(f32[16,64,2,8,64]{4,3,2,1,0:T(8,128)} %bitcast.591) | data formatting | bytes 8388608 | tf_op jit(solution)/shard_map/reshape | solution.py:162
  214.4 33.9 %slice.169 = f32[1023,1024]{1,0:T(8,128)} reverse(f32[1023,1024]{1,0:T(8,128)} %slice.219), dimensions={0} | reverse | bytes 8380416 | tf_op jit(solution)/shard_map/jit(_roll_static)/slice | solution.py:64
  266.1 9.2 %fusion.25 = f32[512,1024]{1,0:T(8,128)} fusion(f32[512,512]{1,0:T(8,128)S(1)} %get-tuple-element.119, f32[512,512]{1,0:T(8,128)S(1)} %get-tuple-element.118, f32[512,1024]{1,0:T(8,128)S(1)} %fusion.24, s32[1024]{0:T(1024)S(1)} %bitcast.604), kind=kLoop, calls=%fused_computation.46 | loop fusion | flops 9437184 | bytes 6295552 | tf_op jit(solution)/shard_map/add | solution.py:78
  293.2 9.5 %copy.641 = f32[512,2,2,8,64]{4,3,2,1,0:T(8,128)} copy(f32[512,2,2,8,64]{0,4,3,2,1:T(8,128)} %pad_maximum_fusion.2) | data formatting | bytes 8388608 | tf_op jit(solution)/shard_map/stack | solution.py:80
  302.7 13.3 %reshape.1845 = f32[16,1,65536]{2,1,0:T(1,128)} reshape(f32[512,2,2,8,64]{4,3,2,1,0:T(8,128)} %copy.641) | data formatting | bytes 8388608
  316.0 19.7 %all-to-all-start.1 = ((f32[16,1,65536]{2,1,0:T(1,128)}), f32[16,1,65536]{2,1,0:T(1,128)}, u32[]{:S(2)}, u32[]{:S(2)}) async-start(f32[16,1,65536]{2,1,0:T(1,128)} %reshape.1845), calls=%async_computation.1 | async-start | bytes 8388608 | tf_op jit(solution)/shard_map/all_to_all | solution.py:167
  336.4 76.9 %all-to-all-done.1 = f32[16,1,65536]{2,1,0:T(1,128)} async-done(((f32[16,1,65536]{2,1,0:T(1,128)}), f32[16,1,65536]{2,1,0:T(1,128)}, u32[]{:S(2)}, u32[]{:S(2)}) %all-to-all-start.1) | async-done | bytes 4194336 | tf_op jit(solution)/shard_map/all_to_all | solution.py:167
  413.3 13.6 %reduce.1 = f32[16,65536]{1,0:T(8,128)} reduce(f32[16,1,65536]{2,1,0:T(1,128)} %all-to-all-done.1, f32[]{:T(128)} %broadcast.1485), dimensions={1}, to_apply=%all_to_all.40.reduce_sub_computation | reduce | bytes 8388612 | tf_op jit(solution)/shard_map/all_to_all | solution.py:167
  427.0 6.9 %reshape.1846 = f32[512,2,2,8,64]{4,3,2,1,0:T(8,128)} reshape(f32[16,65536]{1,0:T(8,128)} %reduce.1) | data formatting | bytes 8388608
  433.9 11.4 %copy.642 = f32[32,2,2,8,16,64]{5,4,3,1,0,2:T(8,128)} copy(f32[32,2,2,8,16,64]{5,3,2,1,0,4:T(8,128)} %bitcast.592) | data formatting | bytes 8388608 | tf_op jit(solution)/shard_map/all_to_all | solution.py:167
  445.3 7.8 %all_to_all.43 = f32[32,2,2,8,1024]{4,3,1,0,2:T(8,128)} reshape(f32[32,2,2,8,16,64]{5,4,3,1,0,2:T(8,128)} %copy.642) | data formatting | bytes 8388608 | tf_op jit(solution)/shard_map/all_to_all | solution.py:167
  503.3 8.5 %reshape.1847 = f32[16,1,32768]{2,1,0:T(1,128)S(1)} reshape(f32[1024,2,2,4,32]{4,3,2,1,0:T(4,128)} %bitcast.588) | data formatting | bytes 4194304
  511.8 66.9 %all_to_all.51 = f32[16,1,32768]{2,1,0:T(1,128)} all-to-all(f32[16,1,32768]{2,1,0:T(1,128)S(1)} %reshape.1847), channel_id=1, replica_groups=mesh['groups'=2,'freq'=16] {'freq'}, dimensions={0} | all-to-all | bytes 4194304 | tf_op jit(solution)/shard_map/all_to_all | solution.py:173
  578.6 7.2 %reduce.2 = f32[16,32768]{1,0:T(8,128)S(1)} reduce(f32[16,1,32768]{2,1,0:T(1,128)} %all_to_all.51, f32[]{:T(128)} %broadcast.1485), dimensions={1}, to_apply=%all_to_all.44.reduce_sub_computation | reduce | bytes 4194308 | tf_op jit(solution)/shard_map/all_to_all | solution.py:173
  592.2 8.5 %copy.677 = f32[32,4,2,2,16,64]{5,0,4,3,2,1:T(8,128)} copy(f32[32,4,2,2,16,64]{0,1,3,2,5,4:T(4,128)} %bitcast.589) | data formatting | bytes 4194304 | tf_op jit(solution)/shard_map/all_to_all | solution.py:173
  (186 shorter events, 142.7 us)
Async XLA Ops:
  56.2 8.9 %copy-start.13 = (s32[8]{0:T(128)S(1)}, s32[8]{0:T(128)}, u32[]{:S(2)}) copy-start(s32[8]{0:T(128)} %param.7) | copy-start | bytes 100
  56.2 85.2 %all-to-all-start = ((f32[16,1,65536]{2,1,0:T(1,128)}), f32[16,1,65536]{2,1,0:T(1,128)}, u32[]{:S(2)}, u32[]{:S(2)}) async-start(f32[16,1,65536]{2,1,0:T(1,128)} %reshape.1843), calls=%async_computation | async-start | bytes 8388608 | tf_op jit(solution)/shard_map/all_to_all | solution.py:161
  209.4 4.9 copy-start.3
  214.4 33.9 %slice-start = ((f32[8,128,1024]{2,0,1:T(8,128)}), f32[4,128,1024]{2,0,1:T(4,128)S(1)}, s32[]{:S(2)}) async-start(f32[8,128,1024]{2,0,1:T(8,128)} %copy-done.3), calls=%async_computation.3 | async-start | bytes 4194304 | tf_op jit(solution)/shard_map/slice | solution.py:65
  249.5 1.3 copy-start.4
  249.5 2.9 copy-start.2
  258.9 4.3 copy-start.12
  262.0 2.0 copy-start.5
  275.3 3.1 copy-start.6
  280.0 5.2 copy-start.8
  280.0 5.2 copy-start.9
  280.0 5.2 copy-start.10
  285.3 5.4 copy-start.7
  316.0 97.4 %all-to-all-start.1 = ((f32[16,1,65536]{2,1,0:T(1,128)}), f32[16,1,65536]{2,1,0:T(1,128)}, u32[]{:S(2)}, u32[]{:S(2)}) async-start(f32[16,1,65536]{2,1,0:T(1,128)} %reshape.1845), calls=%async_computation.1 | async-start | bytes 8388608 | tf_op jit(solution)/shard_map/all_to_all | solution.py:167
  459.5 6.6 %copy-start = (f32[32,2,2,8,1024]{4,3,1,0,2:T(8,128)S(1)}, f32[32,2,2,8,1024]{4,3,1,0,2:T(8,128)}, u32[]{:S(2)}) copy-start(f32[32,2,2,8,1024]{4,3,1,0,2:T(8,128)} %all_to_all.43) | copy-start | bytes 12582916
  483.2 7.1 %copy-start.11 = (f32[32,4]{0,1:T(4,128)}, f32[32,4]{0,1:T(4,128)S(1)}, u32[]{:S(2)}) copy-start(f32[32,4]{0,1:T(4,128)S(1)} %get-tuple-element.137) | copy-start | bytes 1540
  490.3 3.7 copy-start.1
where the time goes:
time: 616 us; the launch traced here: 605 us
  local copies, waits for them, and re-layouts  215 us (35%)
  waiting for transfers between devices  153 us (25%)
  other arithmetic  79.8 us (13%)
  blocking collectives  66.9 us (11%)
  matrix products  60.3 us (10%)
  starting transfers between devices  27.2 us (4%)
    all_to_all x1, waiting for transfers between devices, local(): lax.all_to_all(shaped, 'freq', split_axis=0, concat_axis=4, tiled=True)  76.9 us
    all_to_all x1, waiting for transfers between devices, local(): lax.all_to_all(packed, 'freq', split_axis=3, concat_axis=0, tiled=True)  76.1 us
    unnamed x39, local copies, waits for them, and re-layouts  69.9 us
    all_to_all x1, blocking collectives, local(): lax.all_to_all(local_modes, 'freq', split_axis=4, concat_axis=0, tiled=True)  66.9 us
    slice x3, local copies, waits for them, and re-layouts, unpack_pairs(): mirror = jnp.roll(jnp.flip(spectrum, 0), 1, 0)[:half_bins]  36.3 us
    all_to_all x1, starting transfers between devices, local(): lax.all_to_all(shaped, 'freq', split_axis=0, concat_axis=4, tiled=True)  19.7 us
    all_to_all x2, local copies, waits for them, and re-layouts, local(): lax.all_to_all(shaped, 'freq', split_axis=0, concat_axis=4, tiled=True)  19.2 us
    all_to_all x1, other arithmetic, local(): lax.all_to_all(shaped, 'freq', split_axis=0, concat_axis=4, tiled=True)  13.6 us
  transfers between devices with their start and end apart: 2, of which 2 were waited for; matrix products, arithmetic and copies ran while one was open for 0% of the time, Pallas kernels for 0%

commit v1 on v0

v1 whole, which is shorter than its diff:
```python
import math

import jax
import jax.numpy as jnp
import numpy as np
from jax import lax
from jax.sharding import PartitionSpec as P

MODES = 4
ITERS = 3
precise = lax.Precision.HIGHEST


def transform_table(frames):
    steps = np.arange(frames)
    shape = 0.5 - 0.5 * np.cos(2.0 * np.pi * steps / frames)
    window = shape / np.sqrt(np.sum(shape * shape))
    phase = (steps[:, None] * np.arange(frames // 2)[None, :] % frames) * (2.0 * np.pi / frames)
    table = np.concatenate([np.cos(phase), -np.sin(phase)], axis=1) * window[:, None]
    return table.astype(np.float32)


def phase_table(offsets, bins, frames):
    steps = jnp.arange(bins, dtype=jnp.int32)[None, :] * offsets[:, None] % frames
    angle = steps.astype(jnp.float32) * (2.0 * math.pi / frames)
    return jnp.cos(angle), -jnp.sin(angle)


def sum_over(values, axis):
    size = lax.axis_size(axis)
    if size & (size - 1):
        return lax.psum(values, axis)
    step = 1
    while step < size:
        values = values + lax.ppermute(values, axis, [(i, i ^ step) for i in range(size)])
        step *= 2
    return values


def cmul(a, b):
    return a[0] * b[0] - a[1] * b[1], a[0] * b[1] + a[1] * b[0]


def cdot(a, b):
    return (
        jnp.sum(a[0] * b[0] + a[1] * b[1], axis=0, keepdims=True),
        jnp.sum(a[0] * b[1] - a[1] * b[0], axis=0, keepdims=True),
    )


def times_gram(g, v):
    re = jnp.sum(g[0] * v[0][None] - g[1] * v[1][None], axis=1)
    im = jnp.sum(g[0] * v[1][None] + g[1] * v[0][None], axis=1)
    return re, im


def leading_basis(g):
    blocks, bins = g[0].shape[0], g[0].shape[-1]
    ys = [(g[0][:, m], g[1][:, m]) for m in range(MODES)]
    for sweep in range(ITERS):
        done = []
        for v in ys:
            for q in done:
                part = cmul(cdot(q, v), q)
                v = (v[0] - part[0], v[1] - part[1])
            length = jnp.sqrt(jnp.sum(v[0] * v[0] + v[1] * v[1], axis=0, keepdims=True))
            done.append((v[0] / length, v[1] / length))
        ys = [times_gram(g, q) for q in done]
    energy = jnp.concatenate([cdot(q, y)[0] for q, y in zip(done, ys)], axis=0)
    return done, energy


def local(signal, offsets, pairing, modes_kept):
    rows, blocks, points = signal.shape
    ranks = lax.axis_size("freq")
    rank = lax.axis_index("freq")
    frames = rows * ranks
    bins = frames // 2
    own = points // ranks
    order = pairing.reshape(ranks, own // 2, 2).transpose(0, 2, 1).reshape(-1)
    packed = jnp.take(signal, order, axis=2).reshape(rows, blocks, ranks, own)
    packed = packed.transpose(2, 0, 1, 3)
    series = lax.all_to_all(packed, "freq", split_axis=0, concat_axis=0, tiled=True)
    series = series.reshape(frames, blocks * own)
    table = jnp.asarray(transform_table(frames))
    spectra = lax.dot_general(series, table, (((0,), (0,)), ((), ())), precision=precise)
    spectra = spectra.reshape(blocks, own, 2, bins)
    u = (spectra[:, :, 0], spectra[:, :, 1])
    pairs = []
    for b in range(blocks):
        for e in range(b, blocks):
            pairs.append(jnp.sum(u[0][b] * u[0][e] + u[1][b] * u[1][e], axis=0))
            if e > b:
                pairs.append(jnp.sum(u[0][b] * u[1][e] - u[1][b] * u[0][e], axis=0))
    sums = sum_over(jnp.stack(pairs, axis=0), "freq") * (1.0 / points)
    g_re = [[None] * blocks for _ in range(blocks)]
    g_im = [[None] * blocks for _ in range(blocks)]
    at = 0
    for b in range(blocks):
        for e in range(b, blocks):
            g_re[b][e] = g_re[e][b] = sums[at]
            at += 1
            if e > b:
                g_im[b][e], g_im[e][b] = sums[at], -sums[at]
                at += 1
            else:
                g_im[b][b] = jnp.zeros_like(sums[0])
    g = (
        jnp.stack([jnp.stack(row) for row in g_re]),
        jnp.stack([jnp.stack(row) for row in g_im]),
    )
    turn = phase_table(offsets, bins, frames)
    both = cmul((turn[0][:, None], -turn[1][:, None]), (turn[0][None], turn[1][None]))
    basis, energy = leading_basis(cmul(both, g))
    live = jnp.arange(MODES, dtype=jnp.int32)[:, None] < modes_kept[None, :]
    factor = live.astype(jnp.float32) / jnp.sqrt(energy)
    modes = []
    for m in range(MODES):
        q = cmul(turn, basis[m])
        q = (q[0] * factor[m], q[1] * factor[m])
        re = jnp.sum(u[0] * q[0][:, None] - u[1] * q[1][:, None], axis=0)
        im = jnp.sum(u[0] * q[1][:, None] + u[1] * q[0][:, None], axis=0)
        modes.append(jnp.stack([re, im]))
    modes = jnp.stack(modes).reshape(MODES, 2, 2, own // 2, bins)
    held = lax.dynamic_slice_in_dim(energy, rank * (bins // ranks), bins // ranks, axis=1)
    return held.T, modes.transpose(4, 0, 1, 2, 3)


def solution(mesh):
    placed = (P("freq", None, "groups"), P(), P("groups"), P())
    return jax.shard_map(
        local,
        mesh=mesh,
        in_specs=placed,
        out_specs=(P("freq", "groups"), P(None, None, None, None, ("groups", "freq"))),
        check_vma=False,
    )
```

time: 616 us -> 197 us (0.32); the launches traced: 605 us -> 196 us
  local copies, waits for them, and re-layouts: 215 us -> 45.2 us
  waiting for transfers between devices: 153 us -> 13.9 us
  other arithmetic: 79.8 us -> 13.2 us
  matrix products: 60.3 us -> 17 us
  blocking collectives: 66.9 us -> 99.4 us
  starting transfers between devices: 27.2 us -> 6.61 us
    all_to_all x2 -> x0, waiting for transfers between devices: 153 us -> none  [the longest x1 76.9 us: local(): lax.all_to_all(shaped, 'freq', split_axis=0, concat_axis=4, tiled=True)]
    unnamed x39 -> x24, local copies, waits for them, and re-layouts: 69.9 us -> 10.5 us
    slice x12 -> x6, local copies, waits for them, and re-layouts: 47.3 us -> 0.19 us  [the longest x1 0.09 us: leading_basis(): ys = [(g[0][:, m], g[1][:, m]) for m in range(MODES)]]
    dot_general x28 -> x1, matrix products: 60.3 us -> 17 us  [local(): lax.dot_general(series, table, (((0,), (0,)), ((), ())), precision=precise)]
    all_to_all x5 -> x0, local copies, waits for them, and re-layouts: 38.6 us -> none  [the longest x2 19.2 us: local(): lax.all_to_all(shaped, 'freq', split_axis=0, concat_axis=4, tiled=True)]
    all_to_all x3 -> x0, other arithmetic: 34.5 us -> none  [the longest x1 13.6 us: local(): lax.all_to_all(shaped, 'freq', split_axis=0, concat_axis=4, tiled=True)]
    all_to_all x1, blocking collectives: 66.9 us -> 99.4 us  [local(): lax.all_to_all(packed, 'freq', split_axis=0, concat_axis=0, tiled=True)]
    all_to_all x2 -> x0, starting transfers between devices: 27.2 us -> none  [the longest x1 19.7 us: local(): lax.all_to_all(shaped, 'freq', split_axis=0, concat_axis=4, tiled=True)]
  transfers between devices with their start and end apart: 2 -> 4, of which waited for: 2 -> 4; matrix products, arithmetic and copies ran while one was open for 0% -> 0% of each run, Pallas kernels for 0% -> 0%
where the time goes in v1:
time: 197 us; the launch traced here: 196 us
  blocking collectives  99.4 us (50%)
  local copies, waits for them, and re-layouts  45.2 us (23%)
  matrix products  17 us (9%)
  waiting for transfers between devices  13.9 us (7%)
  other arithmetic  13.2 us (7%)
  starting transfers between devices  6.61 us (3%)
    all_to_all x1, blocking collectives, local(): lax.all_to_all(packed, 'freq', split_axis=0, concat_axis=0, tiled=True)  99.4 us
    gather x2, local copies, waits for them, and re-layouts, local(): packed = jnp.take(signal, order, axis=2).reshape(rows, blocks, ranks, own)  26 us
    dot_general x1, matrix products, local(): lax.dot_general(series, table, (((0,), (0,)), ((), ())), precision=precise)  17 us
    ppermute x4, waiting for transfers between devices, sum_over(): lax.ppermute(values, axis, [(i, i ^ step) for i in range(size)])  13.9 us
    unnamed x24, local copies, waits for them, and re-layouts  10.5 us
    ppermute x4, starting transfers between devices, sum_over(): lax.ppermute(values, axis, [(i, i ^ step) for i in range(size)])  6.61 us
    dot_general x1, local copies, waits for them, and re-layouts, local(): lax.dot_general(series, table, (((0,), (0,)), ((), ())), precision=precise)  5.34 us
  transfers between devices with their start and end apart: 4, of which 4 were waited for; matrix products, arithmetic and copies ran while one was open for 0% of the time, Pallas kernels for 0%

profile of v1, /device:TPU:0, one launch (start us, length us, event | category | flops | bytes accessed | tf_op | source)
XLA Modules:
  0.0 196.5 jit_solution(9319402497872420140)
XLA Ops:
  0.6 1.2 reshape.5963
  2.2 7.5 %copy.42 = f32[64,8,2048]{0,1,2:T(8,128)} copy(f32[64,8,2048]{2,1,0:T(8,128)} %param.5) | data formatting | bytes 8388608 | tf_op args[0]
  9.7 19.2 %gather_fusion = f32[2048,64,8]{1,2,0:T(8,128)} fusion(f32[64,8,2048]{0,1,2:T(8,128)} %copy.42, s32[2048]{0:T(1024)S(1)} %broadcast_clamp_fusion), kind=kCustom, calls=%fused_computation | custom fusion | bytes 8396800 | tf_op jit(solution)/shard_map/jit(_take)/gather | solution.py:81
  28.9 6.8 %copy.43 = f32[64,8,16,128]{3,1,0,2:T(8,128)} copy(f32[64,8,16,128]{0,1,3,2:T(8,128)} %bitcast.249) | data formatting | bytes 8388608 | tf_op jit(solution)/shard_map/jit(_take)/gather | solution.py:81
  35.7 2.5 %select_bitcast_fusion = f32[16,64,8,128]{3,2,1,0:T(8,128)S(1)} fusion(f32[64,8,16,128]{3,1,0,2:T(8,128)} %copy.43, pred[16,128]{1,0:T(8,128)(4,1)S(1)} %compare_and_fusion), kind=kLoop, calls=%fused_computation.2 | loop fusion | flops 1048576 | bytes 8390656 | tf_op jit(solution)/shard_map/transpose | solution.py:82
  38.2 99.4 %all_to_all.5 = f32[16,64,8,128]{3,2,1,0:T(8,128)S(1)} all-to-all(f32[16,64,8,128]{3,2,1,0:T(8,128)S(1)} %select_bitcast_fusion), channel_id=1, replica_groups=mesh['groups'=2,'freq'=16] {'freq'}, dimensions={0} | all-to-all | bytes 8388608 | tf_op jit(solution)/shard_map/all_to_all | solution.py:83
  137.6 2.9 %copy.121 = f32[128,8,8,128]{3,1,2,0:T(8,128)} copy(f32[128,8,8,128]{3,2,1,0:T(8,128)S(1)} %bitcast.250) | data formatting | bytes 8388608
  140.6 5.3 %copy.44 = f32[1024,1024]{1,0:T(8,128)} copy(f32[1024,1024]{0,1:T(8,128)} %bitcast.251) | data formatting | bytes 8388608 | tf_op jit(solution)/shard_map/dot_general | solution.py:86
  145.9 17.0 %fusion.24 = f32[8,128,2,512]{3,1,2,0:T(8,128)S(1)} fusion(f32[8,128,1024,1]{2,1,3,0:T(8,128)} %bitcast.252, f32[2,512,1024,1]{2,1,0,3:T(8,128)} %constant.54), kind=kOutput, calls=%fused_computation.309 | convolution fusion | flops 12884901888 | bytes 12582912 | tf_op jit(solution)/shard_map/dot_general | solution.py:86
  162.9 0.5 add_reduce_fusion.8
  163.3 0.5 add_reduce_fusion.7
  163.9 0.4 subtract_reduce_fusion.6
  165.2 0.5 add_reduce_fusion.6
  167.1 0.8 collective-permute-start
  168.0 1.0 collective-permute-done
  169.0 1.3 collective-permute-start.1
  170.3 4.5 %collective-permute-done.1 = f32[64,512]{1,0:T(8,128)S(1)} collective-permute-done((f32[64,512]{1,0:T(8,128)S(1)}, f32[64,512]{1,0:T(8,128)S(1)}, u32[]{:S(2)}, u32[]{:S(2)}) %collective-permute-start.1) | collective-permute-done | bytes 131104 | tf_op jit(solution)/shard_map/ppermute | solution.py:35
  174.8 1.9 collective-permute-start.2
  176.7 3.2 %collective-permute-done.2 = f32[64,512]{1,0:T(8,128)S(1)} collective-permute-done((f32[64,512]{1,0:T(8,128)S(1)}, f32[64,512]{1,0:T(8,128)S(1)}, u32[]{:S(2)}, u32[]{:S(2)}) %collective-permute-start.2) | collective-permute-done | bytes 131104 | tf_op jit(solution)/shard_map/ppermute | solution.py:35
  180.0 2.5 %collective-permute-start.3 = (f32[64,512]{1,0:T(8,128)S(1)}, f32[64,512]{1,0:T(8,128)S(1)}, u32[]{:S(2)}, u32[]{:S(2)}) collective-permute-start(f32[64,512]{1,0:T(8,128)S(1)} %add.716), channel_id=1, source_target_pairs={{0,8},{1,9},{2,10},{3,11},{4,12},{5,13},{6,14},{7,15},{8,0},{9,1},... | collective-permute-start | bytes 393224 | tf_op jit(solution)/shard_map/ppermute | solution.py:35
  182.7 5.2 %collective-permute-done.3 = f32[64,512]{1,0:T(8,128)S(1)} collective-permute-done((f32[64,512]{1,0:T(8,128)S(1)}, f32[64,512]{1,0:T(8,128)S(1)}, u32[]{:S(2)}, u32[]{:S(2)}) %collective-permute-start.3) | collective-permute-done | bytes 131104 | tf_op jit(solution)/shard_map/ppermute | solution.py:35
  191.5 0.7 dynamic-slice_bitcast_fusion
  192.3 2.6 %subtract_reduce_fusion.3 = (f32[128,512]{1,0:T(8,128)S(1)}, f32[128,512]{1,0:T(8,128)S(1)}, f32[128,512]{1,0:T(8,128)S(1)}, f32[128,512]{1,0:T(8,128)S(1)}, f32...) fusion(f32[8,128,2,512]{3,1,2,0:T(8,128)S(1)} %copy-done.1, ...), kind=kLoop, calls=%fused_computation.13 | loop fusion | flops 16252928 | bytes 6422528 | tf_op jit(solution)/shard_map/reduce_sum | solution.py:121
  195.0 1.5 maximum_bitcast_fusion
  (116 shorter events, 6.3 us)
Async XLA Ops:
  162.9 3.5 %copy-start = (f32[8,128,2,512]{3,1,2,0:T(8,128)}, f32[8,128,2,512]{3,1,2,0:T(8,128)S(1)}, u32[]{:S(2)}) copy-start(f32[8,128,2,512]{3,1,2,0:T(8,128)S(1)} %fusion.24) | copy-start | bytes 12582916
  166.4 16.1 %copy-start.2 = (s32[8]{0:T(128)S(1)}, s32[8]{0:T(128)}, u32[]{:S(2)}) copy-start(s32[8]{0:T(128)} %param.6) | copy-start | bytes 100
  167.1 1.8 collective-permute-start
  169.0 5.8 %collective-permute-start.1 = (f32[64,512]{1,0:T(8,128)S(1)}, f32[64,512]{1,0:T(8,128)S(1)}, u32[]{:S(2)}, u32[]{:S(2)}) collective-permute-start(f32[64,512]{1,0:T(8,128)S(1)} %add.714), channel_id=1, source_target_pairs={{0,2},{1,3},{2,0},{3,1},{4,6},{5,7},{6,4},{7,5},{8,10},{9,11},{10,... | collective-permute-start | bytes 393224 | tf_op jit(solution)/shard_map/ppermute | solution.py:35
  174.8 5.1 %collective-permute-start.2 = (f32[64,512]{1,0:T(8,128)S(1)}, f32[64,512]{1,0:T(8,128)S(1)}, u32[]{:S(2)}, u32[]{:S(2)}) collective-permute-start(f32[64,512]{1,0:T(8,128)S(1)} %add.715), channel_id=1, source_target_pairs={{0,4},{1,5},{2,6},{3,7},{4,0},{5,1},{6,2},{7,3},{8,12},{9,13},{10,... | collective-permute-start | bytes 393224 | tf_op jit(solution)/shard_map/ppermute | solution.py:35
  180.0 7.9 %collective-permute-start.3 = (f32[64,512]{1,0:T(8,128)S(1)}, f32[64,512]{1,0:T(8,128)S(1)}, u32[]{:S(2)}, u32[]{:S(2)}) collective-permute-start(f32[64,512]{1,0:T(8,128)S(1)} %add.716), channel_id=1, source_target_pairs={{0,8},{1,9},{2,10},{3,11},{4,12},{5,13},{6,14},{7,15},{8,0},{9,1},... | collective-permute-start | bytes 393224 | tf_op jit(solution)/shard_map/ppermute | solution.py:35
  189.7 1.7 copy-start.3
  189.9 2.5 %copy-start.1 = (f32[8,128,2,512]{3,1,2,0:T(8,128)S(1)}, f32[8,128,2,512]{3,1,2,0:T(8,128)}, u32[]{:S(2)}) copy-start(f32[8,128,2,512]{3,1,2,0:T(8,128)} %copy-done) | copy-start | bytes 12582916

commit v2 on v1

--- a/solution.py
+++ b/solution.py
@@ -2,8 +2,11 @@
 
 import jax
 import jax.numpy as jnp
+import ml_dtypes
 import numpy as np
 from jax import lax
+from jax.experimental import pallas as pl
+from jax.experimental.pallas import tpu as pltpu
 from jax.sharding import PartitionSpec as P
 
 MODES = 4
@@ -70,6 +73,259 @@
     return done, energy
 
 
+LANES = 128
+GROUP = 4
+VMEM = pltpu.CompilerParams(vmem_limit_bytes=48 * 2**20)
+
+
+def split_table(frames):
+    table = transform_table(frames).reshape(frames, 2, -1, LANES)
+    table = table.transpose(0, 2, 1, 3).reshape(frames, frames)
+    high = table.astype(ml_dtypes.bfloat16)
+    low = (table - high.astype(np.float32)).astype(ml_dtypes.bfloat16)
+    return high, low
+
+
+def two_terms(x):
+    high = x.astype(jnp.bfloat16)
+    return high, (x - high.astype(jnp.float32)).astype(jnp.bfloat16)
+
+
+def three_terms(x):
+    high, rest = x.astype(jnp.bfloat16), None
+    rest = x - high.astype(jnp.float32)
+    mid = rest.astype(jnp.bfloat16)
+    return high, mid, (rest - mid.astype(jnp.float32)).astype(jnp.bfloat16)
+
+
+def dot(a, b):
+    return jnp.dot(a, b, preferred_element_type=jnp.float32)
+
+
+def pack_kernel(blocks, strips, dst, *rest):
+    signals, pairing, rest = rest[:strips], rest[strips], rest[strips + 1 :]
+    outs, one_row = rest[:GROUP], rest[GROUP]
+    step = pl.program_id(0)
+    rows = signals[0].shape[0] // blocks
+    depth = strips * LANES
+
+    @pl.when(step == 0)
+    def _():
+        place = lax.broadcasted_iota(jnp.int32, (LANES, LANES), 1)
+        source = lax.broadcasted_iota(jnp.int32, (LANES, LANES), 0)
+        half = LANES // 2
+        wanted = jnp.where(place < half, 2 * place, 2 * (place - half) + 1)
+        turn = (wanted == source).astype(jnp.float32).astype(jnp.bfloat16)
+        lines = pairing[...]
+        upper = (lines >> 5).astype(jnp.float32).astype(jnp.bfloat16)
+        lower = (lines & 31).astype(jnp.float32).astype(jnp.bfloat16)
+        one_row[...] = (dot(upper, turn) * 32.0 + dot(lower, turn)).astype(jnp.int32)
+
+    x = jnp.concatenate(
+        [
+            jnp.concatenate([strip[pl.ds(b, rows, stride=blocks), :] for strip in signals], axis=1)
+            for b in range(blocks)
+        ],
+        axis=0,
+    )
+    terms = three_terms(x)
+    source = lax.broadcasted_iota(jnp.int32, (depth, LANES), 0) + step * depth
+    for at in range(GROUP):
+        line = one_row[pl.ds(dst[at], 1), :]
+        pick = jnp.where(source == line, 1.0, 0.0).astype(jnp.bfloat16)
+        got = dot(terms[0], pick) + dot(terms[1], pick) + dot(terms[2], pick)
+        for b in range(blocks):
+            part = got[b * rows : (b + 1) * rows]
+            spot = (slice(None), slice(b * LANES, (b + 1) * LANES))
+
+            @pl.when(step == 0)
+            def _():
+                outs[at][spot] = part
+
+            @pl.when(step > 0)
+            def _():
+                outs[at][spot] += part
+
+
+def pack(signal, pairing, dst):
+    rows, blocks, points = signal.shape
+    strips = 4
+    depth = strips * LANES
+    width = blocks * LANES
+    return pl.pallas_call(
+        lambda *refs: pack_kernel(blocks, strips, *refs),
+        grid_spec=pltpu.PrefetchScalarGridSpec(
+            num_scalar_prefetch=1,
+            grid=(points // depth,),
+            in_specs=[
+                pl.BlockSpec((rows * blocks, LANES), lambda i, d, n=n: (0, strips * i + n))
+                for n in range(strips)
+            ]
+            + [pl.BlockSpec((points // LANES, LANES), lambda i, d: (0, 0))],
+            out_specs=[pl.BlockSpec((rows, width), lambda i, d: (0, 0))] * GROUP,
+            scratch_shapes=[pltpu.VMEM((points // LANES, LANES), jnp.int32)],
+        ),
+        out_shape=[jax.ShapeDtypeStruct((rows, width), jnp.float32)] * GROUP,
+        compiler_params=VMEM,
+        cost_estimate=pl.CostEstimate(
+            flops=6 * rows * blocks * points * GROUP * LANES, bytes_accessed=8 * 2**20, transcendentals=0
+        ),
+    )(dst, *[signal.reshape(rows * blocks, points)] * strips, pairing.reshape(-1, LANES))
+
+
+def pair_list(blocks):
+    return [(b, e) for b in range(blocks) for e in range(b, blocks)]
+
+
+def gram_tile(re, im, blocks, gram):
+    own = re.shape[0] // blocks
+    at = 0
+    todo = []
+    for b, e in pair_list(blocks):
+        todo.append((at, b, e))
+        at += 1 if b == e else 2
+    for first in range(0, len(todo), 18):
+        chunk = todo[first : first + 18]
+        used = sorted({b for _, b, _ in chunk} | {e for _, _, e in chunk})
+
+        def body(i, sums):
+            start = pl.multiple_of(i * 8, 8)
+            u = {b: (re[pl.ds(b * own + start, 8), :], im[pl.ds(b * own + start, 8), :]) for b in used}
+            out = []
+            for _, b, e in chunk:
+                (br, bi), (er, ei) = u[b], u[e]
+                out.append(br * er + bi * ei)
+                if b != e:
+                    out.append(br * ei - bi * er)
+            return tuple(s + o for s, o in zip(sums, out))
+
+        count = sum(1 if b == e else 2 for _, b, e in chunk)
+        zero = jnp.zeros((8, re.shape[1]), jnp.float32)
+        sums = lax.fori_loop(0, own // 8, body, (zero,) * count)
+        base = chunk[0][0]
+        for n, value in enumerate(sums):
+            gram[base + n : base + n + 1, :] = jnp.sum(value, axis=0, keepdims=True)
+
+
+def spectra_kernel(blocks, count, more, with_gram, src, *refs):
+    xs, (high, low), refs = refs[:count], refs[count : count + 2], refs[count + 2 :]
+    prev, refs = (refs[:2], refs[2:]) if more else (None, refs)
+    (re, im), refs = refs[:2], refs[2:]
+    gram, refs = (refs[0], refs[1:]) if with_gram else (None, refs)
+    x_high, x_low = refs
+    rows = xs[0].shape[0]
+
+    @pl.when(pl.program_id(0) == 0)
+    def _():
+        for g in range(0, count, GROUP):
+            x = jnp.concatenate([x[...] for x in xs[g : g + GROUP]], axis=0)
+            spot = (slice(None), slice(g * rows, (g + GROUP) * rows))
+            x_high[spot], x_low[spot] = two_terms(x.T)
+
+    def table(ref):
+        return jnp.concatenate(
+            [ref[pl.ds(pl.multiple_of(src[n] * rows, rows), rows), :] for n in range(count)], axis=0
+        )
+
+    w_high, w_low = table(high), table(low)
+    got = dot(x_high[...], w_high) + dot(x_low[...], w_high) + dot(x_high[...], w_low)
+    if more:
+        re[...] = prev[0][...] + got[:, :LANES]
+        im[...] = prev[1][...] + got[:, LANES:]
+    else:
+        re[...] = got[:, :LANES]
+        im[...] = got[:, LANES:]
+    if with_gram:
+        gram_tile(re, im, blocks, gram)
+
+
+def spectra(blocks, xs, src, tables, prev=None, with_gram=False):
+    rows, width = xs[0].shape
+    frames = tables[0].shape[0]
+    bins = frames // 2
+    count = len(xs)
+    held = pl.BlockSpec((width, LANES), lambda i, s: (0, i))
+    shape = jax.ShapeDtypeStruct((width, bins), jnp.float32)
+    in_specs = [pl.BlockSpec((rows, width), lambda i, s: (0, 0))] * count
+    in_specs += [pl.BlockSpec((frames, 2 * LANES), lambda i, s: (0, i))] * 2
+    out_specs, out_shape = [held] * 2, [shape] * 2
+    if prev is not None:
+        in_specs += [held] * 2
+    if with_gram:
+        out_specs.append(pl.BlockSpec((blocks * blocks, LANES), lambda i, s: (0, i)))
+        out_shape.append(jax.ShapeDtypeStruct((blocks * blocks, bins), jnp.float32))
+    return pl.pallas_call(
+        lambda *refs: spectra_kernel(blocks, count, prev is not None, with_gram, *refs),
+        grid_spec=pltpu.PrefetchScalarGridSpec(
+            num_scalar_prefetch=1,
+            grid=(bins // LANES,),
+            in_specs=in_specs,
+            out_specs=out_specs,
+            scratch_shapes=[pltpu.VMEM((width, count * rows), jnp.bfloat16)] * 2,
+        ),
+        out_shape=out_shape,
+        compiler_params=VMEM,
+        cost_estimate=pl.CostEstimate(
+            flops=6 * width * frames * count * rows, bytes_accessed=12 * 2**20, transcendentals=0
+        ),
+    )(src, *xs, *tables, *(prev or ()))
+
+
+def gram_of(u, blocks):
+    pairs = []
+    for b, e in pair_list(blocks):
+        pairs.append(jnp.sum(u[0][b] * u[0][e] + u[1][b] * u[1][e], axis=0))
+        if e > b:
+            pairs.append(jnp.sum(u[0][b] * u[1][e] - u[1][b] * u[0][e], axis=0))
+    return jnp.stack(pairs, axis=0)
+
+
+def plain_spectra(signal, pairing):
+    rows, blocks, points = signal.shape
+    ranks = lax.axis_size("freq")
+    frames, own = rows * ranks, points // ranks
+    order = pairing.reshape(ranks, own // 2, 2).transpose(0, 2, 1).reshape(-1)
+    packed = jnp.take(signal, order, axis=2).reshape(rows, blocks, ranks, own)
+    packed = packed.transpose(2, 0, 1, 3)
+    series = lax.all_to_all(packed, "freq", split_axis=0, concat_axis=0, tiled=True)
+    series = series.reshape(frames, blocks * own)
+    table = jnp.asarray(transform_table(frames))
+    both = lax.dot_general(series, table, (((0,), (0,)), ((), ())), precision=precise)
+    both = both.reshape(blocks, own, 2, frames // 2)
+    u = (both[:, :, 0], both[:, :, 1])
+    return u, gram_of(u, blocks)
+
+
+def tiled_spectra(signal, pairing):
+    rows, blocks, points = signal.shape
+    ranks = lax.axis_size("freq")
+    rank = lax.axis_index("freq")
+    tables = [jnp.asarray(t) for t in split_table(rows * ranks)]
+    near = jnp.arange(GROUP, dtype=jnp.int32)
+    groups = ranks // GROUP
+    order = sorted(range(groups), key=lambda s: (-(s & -2), s & 1)) if groups > 2 else [1, 0]
+    order = order[:-2] + [1, 0] if groups > 2 else order
+    got, last = {}, None
+    for s in order:
+        if last is not None:
+            signal, last = lax.optimization_barrier((signal, last))
+        parts = last = pack(signal, pairing, rank ^ (s * GROUP + near))
+        got[s] = [
+            part if s * GROUP + n == 0 else lax.ppermute(part, "freq", [(i, i ^ (s * GROUP + n)) for i in range(ranks)])
+            for n, part in enumerate(parts)
+        ]
+    own = [0, 1]
+    far = [s for s in order if s not in own]
+    total = spectra(blocks, got[0] + got[1], rank ^ jnp.arange(2 * GROUP, dtype=jnp.int32), tables)
+    for s in far:
+        total = spectra(
+            blocks, got[s], rank ^ (s * GROUP + near), tables, total[:2], with_gram=s == far[-1]
+        )
+    re, im, gram = total
+    shape = (blocks, LANES, -1)
+    return (re.reshape(shape), im.reshape(shape)), gram
+
+
 def local(signal, offsets, pairing, modes_kept):
     rows, blocks, points = signal.shape
     ranks = lax.axis_size("freq")
@@ -77,22 +333,9 @@
     frames = rows * ranks
     bins = frames // 2
     own = points // ranks
-    order = pairing.reshape(ranks, own // 2, 2).transpose(0, 2, 1).reshape(-1)
-    packed = jnp.take(signal, order, axis=2).reshape(rows, blocks, ranks, own)
-    packed = packed.transpose(2, 0, 1, 3)
-    series = lax.all_to_all(packed, "freq", split_axis=0, concat_axis=0, tiled=True)
-    series = series.reshape(frames, blocks * own)
-    table = jnp.asarray(transform_table(frames))
-    spectra = lax.dot_general(series, table, (((0,), (0,)), ((), ())), precision=precise)
-    spectra = spectra.reshape(blocks, own, 2, bins)
-    u = (spectra[:, :, 0], spectra[:, :, 1])
-    pairs = []
-    for b in range(blocks):
-        for e in range(b, blocks):
-            pairs.append(jnp.sum(u[0][b] * u[0][e] + u[1][b] * u[1][e], axis=0))
-            if e > b:
-                pairs.append(jnp.sum(u[0][b] * u[1][e] - u[1][b] * u[0][e], axis=0))
-    sums = sum_over(jnp.stack(pairs, axis=0), "freq") * (1.0 / points)
+    tiled = own == LANES and rows % 64 == 0 and ranks == 4 * GROUP and points % 512 == 0
+    u, gram = (tiled_spectra if tiled else plain_spectra)(signal, pairing)
+    sums = sum_over(gram, "freq") * (1.0 / points)
     g_re = [[None] * blocks for _ in range(blocks)]
     g_im = [[None] * blocks for _ in range(blocks)]
     at = 0

time: 197 us -> 225 us (1.14)
  blocking collectives: 99.4 us -> 0 us
  Pallas kernels: 0 us -> 95.9 us
  starting transfers between devices: 6.61 us -> 64.6 us
  local copies, waits for them, and re-layouts: 45.2 us -> 9.87 us
  waiting for transfers between devices: 13.9 us -> 46.4 us
  matrix products: 17 us -> 0 us
  other arithmetic: 13.2 us -> 6.77 us
    all_to_all x1 -> x0, blocking collectives: 99.4 us -> none  [local(): lax.all_to_all(packed, 'freq', split_axis=0, concat_axis=0, tiled=True)]
    pallas_call x0 -> x7, Pallas kernels: none -> 95.9 us  [the longest x4 72 us: pack(): pl.pallas_call(lambda *refs: pack_kernel(blocks, strips, *refs), grid_spe...]
    ppermute x0 -> x15, starting transfers between devices: none -> 44.1 us  [tiled_spectra(): lax.ppermute(part, 'freq', [(i, i ^ s * GROUP + n) for i in range(ranks)])]
    ppermute x0 -> x15, waiting for transfers between devices: none -> 33.2 us  [tiled_spectra(): lax.ppermute(part, 'freq', [(i, i ^ s * GROUP + n) for i in range(ranks)])]
    gather x2 -> x0, local copies, waits for them, and re-layouts: 26 us -> none  [local(): packed = jnp.take(signal, order, axis=2).reshape(rows, blocks, ranks, own)]
    dot_general x1 -> x0, matrix products: 17 us -> none  [local(): lax.dot_general(series, table, (((0,), (0,)), ((), ())), precision=precise)]
    ppermute x4, starting transfers between devices: 6.61 us -> 20.5 us  [sum_over(): lax.ppermute(values, axis, [(i, i ^ step) for i in range(size)])]
    dot_general x1 -> x0, local copies, waits for them, and re-layouts: 5.34 us -> none  [local(): lax.dot_general(series, table, (((0,), (0,)), ((), ())), precision=precise)]
  transfers between devices with their start and end apart: 4 -> 19, of which waited for: 4 -> 9; matrix products, arithmetic and copies ran while one was open for 0% -> 0% of each run, Pallas kernels for 0% -> 6%
where the time goes in v2:
time: 225 us
  Pallas kernels  95.9 us (43%)
  starting transfers between devices  64.6 us (29%)
  waiting for transfers between devices  46.4 us (21%)
  local copies, waits for them, and re-layouts  9.87 us (4%)
  other arithmetic  6.77 us (3%)
    pallas_call x4, Pallas kernels, pack(): pl.pallas_call(lambda *refs: pack_kernel(blocks, strips, *refs), grid_spe...  72 us
    ppermute x15, starting transfers between devices, tiled_spectra(): lax.ppermute(part, 'freq', [(i, i ^ s * GROUP + n) for i in range(ranks)])  44.1 us
    ppermute x15, waiting for transfers between devices, tiled_spectra(): lax.ppermute(part, 'freq', [(i, i ^ s * GROUP + n) for i in range(ranks)])  33.2 us
    pallas_call x3, Pallas kernels, spectra(): pl.pallas_call(lambda *refs: spectra_kernel(blocks, count, prev is not No...  23.9 us
    ppermute x4, starting transfers between devices, sum_over(): lax.ppermute(values, axis, [(i, i ^ step) for i in range(size)])  20.5 us
    ppermute x4, waiting for transfers between devices, sum_over(): lax.ppermute(values, axis, [(i, i ^ step) for i in range(size)])  13.2 us
    unnamed x34, local copies, waits for them, and re-layouts  8.29 us
  transfers between devices with their start and end apart: 19, of which 9 were waited for; matrix products, arithmetic and copies ran while one was open for 0% of the time, Pallas kernels for 6%

profile of v2, /device:TPU:0, one launch (start us, length us, event | category | flops | bytes accessed | tf_op | source)
XLA Modules:
  0.0 224.8 jit_solution(8872890139901452369)
XLA Ops:
  3.6 18.0 %shard_map.77 = (f32[64,1024]{1,0:T(8,128)S(1)}, f32[64,1024]{1,0:T(8,128)S(1)}, f32[64,1024]{1,0:T(8,128)S(1)}, f32[64,1024]{1,0:T(8,128)S(1)}) custom-call(s32[4]{0:T(128)S(1)} %add_xor_fusion.1.refs_0_, f32[512,2048]{1,0:T(8,128)S(1)} %bitcast.131, f32[512,2048]{1,0:T(8,128)S(1)} %bitcast.132, f32[512,2048]{1,0:T(8,128)S(1)} %bitcast.133, ...), custom_call_target="tpu_custom_call" | custom-call | flops 3221225472 | bytes 8388608 | tf_op jit(solution)/shard_map/pallas_call | solution.py:155
  21.6 18.0 %shard_map.78 = (f32[64,1024]{1,0:T(8,128)S(1)}, f32[64,1024]{1,0:T(8,128)S(1)}, f32[64,1024]{1,0:T(8,128)S(1)}, f32[64,1024]{1,0:T(8,128)S(1)}) custom-call(s32[4]{0:T(128)S(1)} %add_xor_fusion.2.refs_0_, f32[512,2048]{1,0:T(8,128)S(1)} %bitcast.135, f32[512,2048]{1,0:T(8,128)S(1)} %bitcast.136, f32[512,2048]{1,0:T(8,128)S(1)} %bitcast.137, ...), custom_call_target="tpu_custom_call" | custom-call | flops 3221225472 | bytes 8388608 | tf_op jit(solution)/shard_map/pallas_call | solution.py:155
  39.6 18.0 %shard_map.79 = (f32[64,1024]{1,0:T(8,128)S(1)}, f32[64,1024]{1,0:T(8,128)S(1)}, f32[64,1024]{1,0:T(8,128)S(1)}, f32[64,1024]{1,0:T(8,128)S(1)}) custom-call(s32[4]{0:T(128)S(1)} %get-tuple-element.351.refs_0_, f32[512,2048]{1,0:T(8,128)S(1)} %bitcast.139, f32[512,2048]{1,0:T(8,128)S(1)} %bitcast.140, f32[512,2048]{1,0:T(8,128)S(1)} %bitcast.141, ...), custom_call_target="tpu_custom_call" | custom-call | flops 3221225472 | bytes 8388608 | tf_op jit(solution)/shard_map/pallas_call | solution.py:155
  57.6 18.0 %shard_map.80 = (f32[64,1024]{1,0:T(8,128)S(1)}, f32[64,1024]{1,0:T(8,128)S(1)}, f32[64,1024]{1,0:T(8,128)S(1)}, f32[64,1024]{1,0:T(8,128)S(1)}) custom-call(s32[4]{0:T(128)S(1)} %get-tuple-element.352.refs_0_, f32[512,2048]{1,0:T(8,128)S(1)} %bitcast.143, f32[512,2048]{1,0:T(8,128)S(1)} %bitcast.144, f32[512,2048]{1,0:T(8,128)S(1)} %bitcast.145, ...), custom_call_target="tpu_custom_call" | custom-call | flops 3221225472 | bytes 8388608 | tf_op jit(solution)/shard_map/pallas_call | solution.py:155
  75.6 2.4 %collective-permute-start.10 = (f32[64,1024]{1,0:T(8,128)S(1)}, f32[64,1024]{1,0:T(8,128)S(1)}, u32[]{:S(2)}, u32[]{:S(2)}) collective-permute-start(f32[64,1024]{1,0:T(8,128)S(1)} %get-tuple-element.46), channel_id=1, source_target_pairs={{0,3},{1,2},{2,1},{3,0},{4,7},{5,6},{6,5},{7,4},{8,11},{9,10},{10,... | collective-permute-start | bytes 786440 | tf_op jit(solution)/shard_map/ppermute | solution.py:314
  80.9 3.9 %collective-permute-done.10.refs_4_ = f32[64,1024]{1,0:T(8,128)S(1)} collective-permute-done((f32[64,1024]{1,0:T(8,128)S(1)}, f32[64,1024]{1,0:T(8,128)S(1)}, u32[]{:S(2)}, u32[]{:S(2)}) %collective-permute-start.10) | collective-permute-done | bytes 262176 | tf_op jit(solution)/shard_map/ppermute | solution.py:314
  84.8 3.5 %collective-permute-start.13 = (f32[64,1024]{1,0:T(8,128)S(1)}, f32[64,1024]{1,0:T(8,128)S(1)}, u32[]{:S(2)}, u32[]{:S(2)}) collective-permute-start(f32[64,1024]{1,0:T(8,128)S(1)} %get-tuple-element.40), channel_id=1, source_target_pairs={{0,6},{1,7},{2,4},{3,5},{4,2},{5,3},{6,0},{7,1},{8,14},{9,15},{10,... | collective-permute-start | bytes 786440 | tf_op jit(solution)/shard_map/ppermute | solution.py:314
  90.5 3.4 %collective-permute-start.4 = (f32[64,1024]{1,0:T(8,128)S(1)}, f32[64,1024]{1,0:T(8,128)S(1)}, u32[]{:S(2)}, u32[]{:S(2)}) collective-permute-start(f32[64,1024]{1,0:T(8,128)S(1)} %get-tuple-element.28), channel_id=1, source_target_pairs={{0,8},{1,9},{2,10},{3,11},{4,12},{5,13},{6,14},{7,15},{8,0},{9,1},... | collective-permute-start | bytes 786440 | tf_op jit(solution)/shard_map/ppermute | solution.py:314
  94.0 3.3 %collective-permute-start.6 = (f32[64,1024]{1,0:T(8,128)S(1)}, f32[64,1024]{1,0:T(8,128)S(1)}, u32[]{:S(2)}, u32[]{:S(2)}) collective-permute-start(f32[64,1024]{1,0:T(8,128)S(1)} %get-tuple-element.30), channel_id=1, source_target_pairs={{0,10},{1,11},{2,8},{3,9},{4,14},{5,15},{6,12},{7,13},{8,2},{9,3},... | collective-permute-start | bytes 786440 | tf_op jit(solution)/shard_map/ppermute | solution.py:314
  97.2 14.6 %collective-permute-done.13.refs_7_ = f32[64,1024]{1,0:T(8,128)S(1)} collective-permute-done((f32[64,1024]{1,0:T(8,128)S(1)}, f32[64,1024]{1,0:T(8,128)S(1)}, u32[]{:S(2)}, u32[]{:S(2)}) %collective-permute-start.13) | collective-permute-done | bytes 262176 | tf_op jit(solution)/shard_map/ppermute | solution.py:314
  111.9 3.1 %collective-permute-done.14.refs_8_ = f32[64,1024]{1,0:T(8,128)S(1)} collective-permute-done((f32[64,1024]{1,0:T(8,128)S(1)}, f32[64,1024]{1,0:T(8,128)S(1)}, u32[]{:S(2)}, u32[]{:S(2)}) %collective-permute-start.14) | collective-permute-done | bytes 262176 | tf_op jit(solution)/shard_map/ppermute | solution.py:314
  116.2 2.9 %collective-permute-start.1 = (f32[64,1024]{1,0:T(8,128)S(1)}, f32[64,1024]{1,0:T(8,128)S(1)}, u32[]{:S(2)}, u32[]{:S(2)}) collective-permute-start(f32[64,1024]{1,0:T(8,128)S(1)} %get-tuple-element.34), channel_id=1, source_target_pairs={{0,13},{1,12},{2,15},{3,14},{4,9},{5,8},{6,11},{7,10},{8,5},{9,4},... | collective-permute-start | bytes 786440 | tf_op jit(solution)/shard_map/ppermute | solution.py:314
  119.2 24.5 %collective-permute-start.2 = (f32[64,1024]{1,0:T(8,128)S(1)}, f32[64,1024]{1,0:T(8,128)S(1)}, u32[]{:S(2)}, u32[]{:S(2)}) collective-permute-start(f32[64,1024]{1,0:T(8,128)S(1)} %get-tuple-element.35), channel_id=1, source_target_pairs={{0,14},{1,15},{2,12},{3,13},{4,10},{5,11},{6,8},{7,9},{8,6},{9,7},... | collective-permute-start | bytes 786440 | tf_op jit(solution)/shard_map/ppermute | solution.py:314
  143.6 9.3 %collective-permute-done.6.refs_3_ = f32[64,1024]{1,0:T(8,128)S(1)} collective-permute-done((f32[64,1024]{1,0:T(8,128)S(1)}, f32[64,1024]{1,0:T(8,128)S(1)}, u32[]{:S(2)}, u32[]{:S(2)}) %collective-permute-start.6) | collective-permute-done | bytes 262176 | tf_op jit(solution)/shard_map/ppermute | solution.py:314
  152.9 8.0 %shard_map.81 = (f32[1024,512]{1,0:T(8,128)S(1)}, f32[1024,512]{1,0:T(8,128)}) custom-call(s32[8]{0:T(128)S(1)} %iota_xor_fusion.1.refs_0_, f32[64,1024]{1,0:T(8,128)S(1)} %get-tuple-element.43.refs_1_, f32[64,1024]{1,0:T(8,128)S(1)} %collective-permute-done.8.refs_2_, f32[64,1024]{1,0:T(8,128)S(1)} %collective-permute-done.9.refs_3_, ...), custom_call_target="tpu_custom_call" | custom-call | flops 3221225472 | bytes 12582912 | tf_op jit(solution)/shard_map/pallas_call | solution.py:257
  162.3 6.3 %shard_map.82 = (f32[1024,512]{1,0:T(8,128)S(1)}, f32[1024,512]{1,0:T(8,128)S(1)}) custom-call(s32[4]{0:T(128)S(1)} %add_xor_fusion.1.refs_0_, f32[64,1024]{1,0:T(8,128)S(1)} %collective-permute-done.4.refs_1_, f32[64,1024]{1,0:T(8,128)S(1)} %collective-permute-done.5.refs_2_, f32[64,1024]{1,0:T(8,128)S(1)} %collective-permute-done.6.refs_3_, ...), custom_call_target="tpu_custom_call" | custom-call | flops 1610612736 | bytes 12582912 | tf_op jit(solution)/shard_map/pallas_call | solution.py:257
  171.3 9.6 %shard_map.83 = (f32[1024,512]{1,0:T(8,128)S(1)}, f32[1024,512]{1,0:T(8,128)S(1)}, f32[64,512]{1,0:T(8,128)S(1)}) custom-call(s32[4]{0:T(128)S(1)} %add_xor_fusion.2.refs_0_, f32[64,1024]{1,0:T(8,128)S(1)} %collective-permute-done.refs_1_, f32[64,1024]{1,0:T(8,128)S(1)} %collective-permute-done.1.refs_2_, f32[64,1024]{1,0:T(8,128)S(1)} %collective-permute-done.2.refs_3_, ...), custom_call_target="tpu_custom_call" | custom-call | flops 1610612736 | bytes 12582912 | tf_op jit(solution)/shard_map/pallas_call | solution.py:257
  182.3 3.7 %collective-permute-start.15 = (f32[64,512]{1,0:T(8,128)S(1)}, f32[64,512]{1,0:T(8,128)S(1)}, u32[]{:S(2)}, u32[]{:S(2)}) collective-permute-start(f32[64,512]{1,0:T(8,128)S(1)} %get-tuple-element.51), channel_id=1, source_target_pairs={{0,1},{1,0},{2,3},{3,2},{4,5},{5,4},{6,7},{7,6},{8,9},{9,8},{10,11... | collective-permute-start | bytes 393224 | tf_op jit(solution)/shard_map/ppermute | solution.py:38
  188.5 4.3 %collective-permute-done.16 = f32[64,512]{1,0:T(8,128)S(1)} collective-permute-done((f32[64,512]{1,0:T(8,128)S(1)}, f32[64,512]{1,0:T(8,128)S(1)}, u32[]{:S(2)}, u32[]{:S(2)}) %collective-permute-start.16) | collective-permute-done | bytes 131104 | tf_op jit(solution)/shard_map/ppermute | solution.py:38
  192.8 11.2 %collective-permute-start.17 = (f32[64,512]{1,0:T(8,128)S(1)}, f32[64,512]{1,0:T(8,128)S(1)}, u32[]{:S(2)}, u32[]{:S(2)}) collective-permute-start(f32[64,512]{1,0:T(8,128)S(1)} %add.523), channel_id=1, source_target_pairs={{0,4},{1,5},{2,6},{3,7},{4,0},{5,1},{6,2},{7,3},{8,12},{9,13},{10,... | collective-permute-start | bytes 393224 | tf_op jit(solution)/shard_map/ppermute | solution.py:38
  204.1 3.2 %collective-permute-done.17 = f32[64,512]{1,0:T(8,128)S(1)} collective-permute-done((f32[64,512]{1,0:T(8,128)S(1)}, f32[64,512]{1,0:T(8,128)S(1)}, u32[]{:S(2)}, u32[]{:S(2)}) %collective-permute-start.17) | collective-permute-done | bytes 131104 | tf_op jit(solution)/shard_map/ppermute | solution.py:38
  207.3 4.0 %collective-permute-start.18 = (f32[64,512]{1,0:T(8,128)S(1)}, f32[64,512]{1,0:T(8,128)S(1)}, u32[]{:S(2)}, u32[]{:S(2)}) collective-permute-start(f32[64,512]{1,0:T(8,128)S(1)} %add.524), channel_id=1, source_target_pairs={{0,8},{1,9},{2,10},{3,11},{4,12},{5,13},{6,14},{7,15},{8,0},{9,1},... | collective-permute-start | bytes 393224 | tf_op jit(solution)/shard_map/ppermute | solution.py:38
  211.4 4.7 %collective-permute-done.18 = f32[64,512]{1,0:T(8,128)S(1)} collective-permute-done((f32[64,512]{1,0:T(8,128)S(1)}, f32[64,512]{1,0:T(8,128)S(1)}, u32[]{:S(2)}, u32[]{:S(2)}) %collective-permute-start.18) | collective-permute-done | bytes 131104 | tf_op jit(solution)/shard_map/ppermute | solution.py:38
  220.6 2.6 %subtract_reduce_fusion.3 = (f32[128,512]{1,0:T(8,128)S(1)}, f32[128,512]{1,0:T(8,128)S(1)}, f32[128,512]{1,0:T(8,128)S(1)}, f32[128,512]{1,0:T(8,128)S(1)}, f32...) fusion(f32[8,128,512]{2,1,0:T(8,128)S(1)} %bitcast.148, ...), kind=kLoop, calls=%fused_computation.8 | loop fusion | flops 16252928 | bytes 6422528 | tf_op jit(solution)/shard_map/reduce_sum | solution.py:364
  (145 shorter events, 23.0 us)
Async XLA Ops:
  0.7 2.2 copy-start
  3.6 18.0 %copy-start.1 = (f32[64,8,2048]{2,1,0:T(8,128)S(1)}, f32[64,8,2048]{2,1,0:T(8,128)}, u32[]{:S(2)}) copy-start(f32[64,8,2048]{2,1,0:T(8,128)} %param.6) | copy-start | bytes 12582916
  75.6 9.1 %collective-permute-start.10 = (f32[64,1024]{1,0:T(8,128)S(1)}, f32[64,1024]{1,0:T(8,128)S(1)}, u32[]{:S(2)}, u32[]{:S(2)}) collective-permute-start(f32[64,1024]{1,0:T(8,128)S(1)} %get-tuple-element.46), channel_id=1, source_target_pairs={{0,3},{1,2},{2,1},{3,0},{4,7},{5,6},{6,5},{7,4},{8,11},{9,10},{10,... | collective-permute-start | bytes 786440 | tf_op jit(solution)/shard_map/ppermute | solution.py:314
  78.1 10.2 %collective-permute-start.8 = (f32[64,1024]{1,0:T(8,128)S(1)}, f32[64,1024]{1,0:T(8,128)S(1)}, u32[]{:S(2)}, u32[]{:S(2)}) collective-permute-start(f32[64,1024]{1,0:T(8,128)S(1)} %get-tuple-element.44), channel_id=1, source_target_pairs={{0,1},{1,0},{2,3},{3,2},{4,5},{5,4},{6,7},{7,6},{8,9},{9,8},{10,11... | collective-permute-start | bytes 786440 | tf_op jit(solution)/shard_map/ppermute | solution.py:314
  78.7 11.8 %collective-permute-start.9 = (f32[64,1024]{1,0:T(8,128)S(1)}, f32[64,1024]{1,0:T(8,128)S(1)}, u32[]{:S(2)}, u32[]{:S(2)}) collective-permute-start(f32[64,1024]{1,0:T(8,128)S(1)} %get-tuple-element.45), channel_id=1, source_target_pairs={{0,2},{1,3},{2,0},{3,1},{4,6},{5,7},{6,4},{7,5},{8,10},{9,11},{10,... | collective-permute-start | bytes 786440 | tf_op jit(solution)/shard_map/ppermute | solution.py:314
  78.8 15.2 %collective-permute-start.11 = (f32[64,1024]{1,0:T(8,128)S(1)}, f32[64,1024]{1,0:T(8,128)S(1)}, u32[]{:S(2)}, u32[]{:S(2)}) collective-permute-start(f32[64,1024]{1,0:T(8,128)S(1)} %get-tuple-element.38), channel_id=1, source_target_pairs={{0,4},{1,5},{2,6},{3,7},{4,0},{5,1},{6,2},{7,3},{8,12},{9,13},{10,... | collective-permute-start | bytes 786440 | tf_op jit(solution)/shard_map/ppermute | solution.py:314
  80.9 13.1 %collective-permute-start.12 = (f32[64,1024]{1,0:T(8,128)S(1)}, f32[64,1024]{1,0:T(8,128)S(1)}, u32[]{:S(2)}, u32[]{:S(2)}) collective-permute-start(f32[64,1024]{1,0:T(8,128)S(1)} %get-tuple-element.39), channel_id=1, source_target_pairs={{0,5},{1,4},{2,7},{3,6},{4,1},{5,0},{6,3},{7,2},{8,13},{9,12},{10,... | collective-permute-start | bytes 786440 | tf_op jit(solution)/shard_map/ppermute | solution.py:314
  84.8 27.1 %collective-permute-start.13 = (f32[64,1024]{1,0:T(8,128)S(1)}, f32[64,1024]{1,0:T(8,128)S(1)}, u32[]{:S(2)}, u32[]{:S(2)}) collective-permute-start(f32[64,1024]{1,0:T(8,128)S(1)} %get-tuple-element.40), channel_id=1, source_target_pairs={{0,6},{1,7},{2,4},{3,5},{4,2},{5,3},{6,0},{7,1},{8,14},{9,15},{10,... | collective-permute-start | bytes 786440 | tf_op jit(solution)/shard_map/ppermute | solution.py:314
  88.2 26.7 %collective-permute-start.14 = (f32[64,1024]{1,0:T(8,128)S(1)}, f32[64,1024]{1,0:T(8,128)S(1)}, u32[]{:S(2)}, u32[]{:S(2)}) collective-permute-start(f32[64,1024]{1,0:T(8,128)S(1)} %get-tuple-element.41), channel_id=1, source_target_pairs={{0,7},{1,6},{2,5},{3,4},{4,3},{5,2},{6,1},{7,0},{8,15},{9,14},{10,... | collective-permute-start | bytes 786440 | tf_op jit(solution)/shard_map/ppermute | solution.py:314
  90.5 25.7 %collective-permute-start.4 = (f32[64,1024]{1,0:T(8,128)S(1)}, f32[64,1024]{1,0:T(8,128)S(1)}, u32[]{:S(2)}, u32[]{:S(2)}) collective-permute-start(f32[64,1024]{1,0:T(8,128)S(1)} %get-tuple-element.28), channel_id=1, source_target_pairs={{0,8},{1,9},{2,10},{3,11},{4,12},{5,13},{6,14},{7,15},{8,0},{9,1},... | collective-permute-start | bytes 786440 | tf_op jit(solution)/shard_map/ppermute | solution.py:314
  94.0 25.2 %collective-permute-start.5 = (f32[64,1024]{1,0:T(8,128)S(1)}, f32[64,1024]{1,0:T(8,128)S(1)}, u32[]{:S(2)}, u32[]{:S(2)}) collective-permute-start(f32[64,1024]{1,0:T(8,128)S(1)} %get-tuple-element.29), channel_id=1, source_target_pairs={{0,9},{1,8},{2,11},{3,10},{4,13},{5,12},{6,15},{7,14},{8,1},{9,0},... | collective-permute-start | bytes 786440 | tf_op jit(solution)/shard_map/ppermute | solution.py:314
  94.0 59.0 %collective-permute-start.6 = (f32[64,1024]{1,0:T(8,128)S(1)}, f32[64,1024]{1,0:T(8,128)S(1)}, u32[]{:S(2)}, u32[]{:S(2)}) collective-permute-start(f32[64,1024]{1,0:T(8,128)S(1)} %get-tuple-element.30), channel_id=1, source_target_pairs={{0,10},{1,11},{2,8},{3,9},{4,14},{5,15},{6,12},{7,13},{8,2},{9,3},... | collective-permute-start | bytes 786440 | tf_op jit(solution)/shard_map/ppermute | solution.py:314
  111.9 50.4 %collective-permute-start.7 = (f32[64,1024]{1,0:T(8,128)S(1)}, f32[64,1024]{1,0:T(8,128)S(1)}, u32[]{:S(2)}, u32[]{:S(2)}) collective-permute-start(f32[64,1024]{1,0:T(8,128)S(1)} %get-tuple-element.31), channel_id=1, source_target_pairs={{0,11},{1,10},{2,9},{3,8},{4,15},{5,14},{6,13},{7,12},{8,3},{9,2},... | collective-permute-start | bytes 786440 | tf_op jit(solution)/shard_map/ppermute | solution.py:314
  114.9 56.4 %collective-permute-start = (f32[64,1024]{1,0:T(8,128)S(1)}, f32[64,1024]{1,0:T(8,128)S(1)}, u32[]{:S(2)}, u32[]{:S(2)}) collective-permute-start(f32[64,1024]{1,0:T(8,128)S(1)} %get-tuple-element.33), channel_id=1, source_target_pairs={{0,12},{1,13},{2,14},{3,15},{4,8},{5,9},{6,10},{7,11},{8,4},{9,5},... | collective-permute-start | bytes 786440 | tf_op jit(solution)/shard_map/ppermute | solution.py:314
  116.2 55.0 %collective-permute-start.1 = (f32[64,1024]{1,0:T(8,128)S(1)}, f32[64,1024]{1,0:T(8,128)S(1)}, u32[]{:S(2)}, u32[]{:S(2)}) collective-permute-start(f32[64,1024]{1,0:T(8,128)S(1)} %get-tuple-element.34), channel_id=1, source_target_pairs={{0,13},{1,12},{2,15},{3,14},{4,9},{5,8},{6,11},{7,10},{8,5},{9,4},... | collective-permute-start | bytes 786440 | tf_op jit(solution)/shard_map/ppermute | solution.py:314
  119.2 52.1 %collective-permute-start.2 = (f32[64,1024]{1,0:T(8,128)S(1)}, f32[64,1024]{1,0:T(8,128)S(1)}, u32[]{:S(2)}, u32[]{:S(2)}) collective-permute-start(f32[64,1024]{1,0:T(8,128)S(1)} %get-tuple-element.35), channel_id=1, source_target_pairs={{0,14},{1,15},{2,12},{3,13},{4,10},{5,11},{6,8},{7,9},{8,6},{9,7},... | collective-permute-start | bytes 786440 | tf_op jit(solution)/shard_map/ppermute | solution.py:314
  152.9 18.3 %collective-permute-start.3 = (f32[64,1024]{1,0:T(8,128)S(1)}, f32[64,1024]{1,0:T(8,128)S(1)}, u32[]{:S(2)}, u32[]{:S(2)}) collective-permute-start(f32[64,1024]{1,0:T(8,128)S(1)} %get-tuple-element.36), channel_id=1, source_target_pairs={{0,15},{1,14},{2,13},{3,12},{4,11},{5,10},{6,9},{7,8},{8,7},{9,6},... | collective-permute-start | bytes 786440 | tf_op jit(solution)/shard_map/ppermute | solution.py:314
  171.3 40.0 %copy-start.8 = (s32[8]{0:T(128)S(1)}, s32[8]{0:T(128)}, u32[]{:S(2)}) copy-start(s32[8]{0:T(128)} %param.7) | copy-start | bytes 100
  182.3 4.7 %collective-permute-start.15 = (f32[64,512]{1,0:T(8,128)S(1)}, f32[64,512]{1,0:T(8,128)S(1)}, u32[]{:S(2)}, u32[]{:S(2)}) collective-permute-start(f32[64,512]{1,0:T(8,128)S(1)} %get-tuple-element.51), channel_id=1, source_target_pairs={{0,1},{1,0},{2,3},{3,2},{4,5},{5,4},{6,7},{7,6},{8,9},{9,8},{10,11... | collective-permute-start | bytes 393224 | tf_op jit(solution)/shard_map/ppermute | solution.py:38
  187.0 5.8 %collective-permute-start.16 = (f32[64,512]{1,0:T(8,128)S(1)}, f32[64,512]{1,0:T(8,128)S(1)}, u32[]{:S(2)}, u32[]{:S(2)}) collective-permute-start(f32[64,512]{1,0:T(8,128)S(1)} %add.522), channel_id=1, source_target_pairs={{0,2},{1,3},{2,0},{3,1},{4,6},{5,7},{6,4},{7,5},{8,10},{9,11},{10,... | collective-permute-start | bytes 393224 | tf_op jit(solution)/shard_map/ppermute | solution.py:38
  192.8 14.5 %collective-permute-start.17 = (f32[64,512]{1,0:T(8,128)S(1)}, f32[64,512]{1,0:T(8,128)S(1)}, u32[]{:S(2)}, u32[]{:S(2)}) collective-permute-start(f32[64,512]{1,0:T(8,128)S(1)} %add.523), channel_id=1, source_target_pairs={{0,4},{1,5},{2,6},{3,7},{4,0},{5,1},{6,2},{7,3},{8,12},{9,13},{10,... | collective-permute-start | bytes 393224 | tf_op jit(solution)/shard_map/ppermute | solution.py:38
  207.3 8.8 %collective-permute-start.18 = (f32[64,512]{1,0:T(8,128)S(1)}, f32[64,512]{1,0:T(8,128)S(1)}, u32[]{:S(2)}, u32[]{:S(2)}) collective-permute-start(f32[64,512]{1,0:T(8,128)S(1)} %add.524), channel_id=1, source_target_pairs={{0,8},{1,9},{2,10},{3,11},{4,12},{5,13},{6,14},{7,15},{8,0},{9,1},... | collective-permute-start | bytes 393224 | tf_op jit(solution)/shard_map/ppermute | solution.py:38
  218.0 1.7 copy-start.9
  218.1 2.5 %copy-start.3 = (f32[1024,512]{1,0:T(8,128)S(1)}, f32[1024,512]{1,0:T(8,128)}, u32[]{:S(2)}) copy-start(f32[1024,512]{1,0:T(8,128)} %copy-done.2) | copy-start | bytes 6291460
  (5 other events, 6.0 us)

commit v3 on v1

--- a/solution.py
+++ b/solution.py
@@ -2,8 +2,11 @@
 
 import jax
 import jax.numpy as jnp
+import ml_dtypes
 import numpy as np
 from jax import lax
+from jax.experimental import pallas as pl
+from jax.experimental.pallas import tpu as pltpu
 from jax.sharding import PartitionSpec as P
 
 MODES = 4
@@ -70,7 +73,334 @@
     return done, energy
 
 
-def local(signal, offsets, pairing, modes_kept):
+LANES = 128
+GROUP = 4
+VMEM = pltpu.CompilerParams(vmem_limit_bytes=60 * 2**20)
+SMALL = pltpu.CompilerParams(vmem_limit_bytes=32 * 2**20)
+
+
+def split_table(frames):
+    table = transform_table(frames).reshape(frames, 2, -1, LANES)
+    table = table.transpose(0, 2, 1, 3).reshape(frames, frames)
+    high = table.astype(ml_dtypes.bfloat16)
+    low = (table - high.astype(np.float32)).astype(ml_dtypes.bfloat16)
+    return high, low
+
+
+def two_terms(x):
+    high = x.astype(jnp.bfloat16)
+    return high, (x - high.astype(jnp.float32)).astype(jnp.bfloat16)
+
+
+def three_terms(x):
+    high, rest = x.astype(jnp.bfloat16), None
+    rest = x - high.astype(jnp.float32)
+    mid = rest.astype(jnp.bfloat16)
+    return high, mid, (rest - mid.astype(jnp.float32)).astype(jnp.bfloat16)
+
+
+def dot(a, b):
+    return jnp.dot(a, b, preferred_element_type=jnp.float32)
+
+
+def pack_kernel(blocks, first, count, strips, *refs):
+    signals, pairing, out, one_row, total = refs[:strips], *refs[strips:]
+    step = pl.program_id(0)
+    rows = signals[0].shape[0] // blocks
+    ranks = out.shape[0]
+    depth = strips * LANES
+
+    @pl.when(step == 0)
+    def _():
+        place = lax.broadcasted_iota(jnp.int32, (LANES, LANES), 1)
+        source = lax.broadcasted_iota(jnp.int32, (LANES, LANES), 0)
+        half = LANES // 2
+        wanted = jnp.where(place < half, 2 * place, 2 * (place - half) + 1)
+        turn = (wanted == source).astype(jnp.float32).astype(jnp.bfloat16)
+        lines = pairing[...]
+        upper = (lines >> 5).astype(jnp.float32).astype(jnp.bfloat16)
+        lower = (lines & 31).astype(jnp.float32).astype(jnp.bfloat16)
+        one_row[...] = (dot(upper, turn) * 32.0 + dot(lower, turn)).astype(jnp.int32)
+        total[...] = jnp.zeros_like(total)
+
+    x = jnp.concatenate(
+        [
+            jnp.concatenate([strip[pl.ds(b, rows, stride=blocks), :] for strip in signals], axis=1)
+            for b in range(first, first + count)
+        ],
+        axis=0,
+    )
+    terms = three_terms(x)
+    source = lax.broadcasted_iota(jnp.int32, (depth, LANES), 0) + step * depth
+    for at in range(0, ranks, GROUP):
+        pick = jnp.concatenate(
+            [
+                jnp.where(source == one_row[n : n + 1, :], 1.0, 0.0).astype(jnp.bfloat16)
+                for n in range(at, at + GROUP)
+            ],
+            axis=1,
+        )
+        spot = (slice(None), slice(at * LANES, (at + GROUP) * LANES))
+        total[spot] += dot(terms[0], pick) + dot(terms[1], pick) + dot(terms[2], pick)
+
+    @pl.when(step == pl.num_programs(0) - 1)
+    def _():
+        for n in range(ranks):
+            for b in range(count):
+                out[n, :, b * LANES : (b + 1) * LANES] = total[
+                    b * rows : (b + 1) * rows, n * LANES : (n + 1) * LANES
+                ]
+
+
+def pack(signal, pairing, first, count):
+    rows, blocks, points = signal.shape
+    strips = 4
+    ranks = points // LANES
+    shape = (ranks, rows, count * LANES)
+    return pl.pallas_call(
+        lambda *refs: pack_kernel(blocks, first, count, strips, *refs),
+        grid=(points // (strips * LANES),),
+        in_specs=[
+            pl.BlockSpec((rows * blocks, LANES), lambda i, n=n: (0, strips * i + n))
+            for n in range(strips)
+        ]
+        + [pl.BlockSpec((ranks, LANES), lambda i: (0, 0))],
+        out_specs=pl.BlockSpec(shape, lambda i: (0, 0, 0)),
+        scratch_shapes=[
+            pltpu.VMEM((ranks, LANES), jnp.int32),
+            pltpu.VMEM((rows * count, points), jnp.float32),
+        ],
+        out_shape=jax.ShapeDtypeStruct(shape, jnp.float32),
+        compiler_params=VMEM,
+        cost_estimate=pl.CostEstimate(
+            flops=6 * rows * count * points * points, bytes_accessed=8 * 2**20, transcendentals=0
+        ),
+    )(*[signal.reshape(rows * blocks, points)] * strips, pairing.reshape(-1, LANES))
+
+
+def pair_list(blocks):
+    return [(b, e) for b in range(blocks) for e in range(b, blocks)]
+
+
+def gram_tile(parts, blocks, gram):
+    where = []
+    for re, im in parts:
+        where += [(re, im, n * LANES) for n in range(re.shape[0] // LANES)]
+    fresh = len(where)
+    start = fresh - parts[-1][0].shape[0] // LANES
+    todo = [(b, e) for e in range(start, fresh) for b in range(e + 1)]
+    most = 14
+    for first in range(0, len(todo), most):
+        chunk = todo[first : first + most]
+        used = sorted({b for b, _ in chunk} | {e for _, e in chunk})
+
+        def body(i, sums):
+            spot = pl.multiple_of(i * 8, 8)
+            u = {}
+            for b in used:
+                re, im, base = where[b]
+                u[b] = (re[pl.ds(base + spot, 8), :], im[pl.ds(base + spot, 8), :])
+            out = []
+            for b, e in chunk:
+                (br, bi), (er, ei) = u[b], u[e]
+                out.append(br * er + bi * ei)
+                if b != e:
+                    out.append(br * ei - bi * er)
+            return tuple(s + o for s, o in zip(sums, out))
+
+        rows = []
+        for b, e in chunk:
+            rows += [e * blocks + b] if b == e else [e * blocks + b, b * blocks + e]
+        zero = jnp.zeros((8, gram.shape[1]), jnp.float32)
+        sums = lax.fori_loop(0, LANES // 8, body, (zero,) * len(rows))
+        for row, value in zip(rows, sums):
+            gram[row : row + 1, :] = jnp.sum(value, axis=0, keepdims=True)
+
+
+def spectra_kernel(blocks, others, final, core, x, high, low, *refs):
+    parts = [(refs[2 * n], refs[2 * n + 1]) for n in range(others)]
+    refs = refs[2 * others :]
+    before, refs = (refs[0], refs[1:]) if others else (None, refs)
+    (re, im), grams, (x_high, x_low, gram) = refs[:2], refs[2:-3], refs[-3:]
+    step = pl.program_id(0)
+
+    @pl.when(step == 0)
+    def _():
+        x_high[...], x_low[...] = two_terms(x[...].T)
+
+    got = dot(x_high[...], high[...]) + dot(x_low[...], high[...]) + dot(x_high[...], low[...])
+    re[...] = got[:, :LANES]
+    im[...] = got[:, LANES:]
+    gram[...] = before[...] if others else jnp.zeros_like(gram)
+    gram_tile(parts + [(re, im)], blocks, gram)
+    if final:
+        half = step // (pl.num_programs(0) // 2)
+        lane = pl.multiple_of(step % (pl.num_programs(0) // 2) * LANES, LANES)
+
+        @pl.when(half == core[0])
+        def _():
+            grams[0][:, pl.ds(lane, LANES)] = gram[...]
+
+        @pl.when(half != core[0])
+        def _():
+            grams[1][:, pl.ds(lane, LANES)] = gram[...]
+    else:
+        grams[0][...] = gram[...]
+
+
+def spectra(blocks, x, tables, core, others=(), before=None, final=False):
+    frames, width = x.shape
+    bins = frames // 2
+    held = pl.BlockSpec((width, LANES), lambda i, c: (0, i))
+    shape = jax.ShapeDtypeStruct((width, bins), jnp.float32)
+    flat = [a for part in others for a in part] + ([before] if others else [])
+    in_specs = [pl.BlockSpec((frames, width), lambda i, c: (0, 0))]
+    in_specs += [pl.BlockSpec((frames, 2 * LANES), lambda i, c: (0, i))] * 2
+    in_specs += [pl.BlockSpec((a.shape[0], LANES), lambda i, c: (0, i)) for a in flat]
+    square = blocks * blocks
+    if final:
+        out_specs = [held] * 2 + [pl.BlockSpec((square, bins // 2), lambda i, c: (0, 0))] * 2
+        out_shape = [shape] * 2 + [jax.ShapeDtypeStruct((square, bins // 2), jnp.float32)] * 2
+    else:
+        out_specs = [held] * 2 + [pl.BlockSpec((square, LANES), lambda i, c: (0, i))]
+        out_shape = [shape] * 2 + [jax.ShapeDtypeStruct((square, bins), jnp.float32)]
+    return pl.pallas_call(
+        lambda *refs: spectra_kernel(blocks, len(others), final, *refs),
+        grid_spec=pltpu.PrefetchScalarGridSpec(
+            num_scalar_prefetch=1,
+            grid=(bins // LANES,),
+            in_specs=in_specs,
+            out_specs=out_specs,
+            scratch_shapes=[pltpu.VMEM((width, frames), jnp.bfloat16)] * 2
+            + [pltpu.VMEM((square, LANES), jnp.float32)],
+        ),
+        out_shape=out_shape,
+        compiler_params=SMALL,
+        cost_estimate=pl.CostEstimate(
+            flops=6 * width * frames * frames, bytes_accessed=12 * 2**20, transcendentals=0
+        ),
+    )(core, x, *tables, *flat)
+
+
+def row_dot(a, b):
+    return (
+        jnp.sum(a[0] * b[0] + a[1] * b[1], axis=0, keepdims=True),
+        jnp.sum(a[0] * b[1] - a[1] * b[0], axis=0, keepdims=True),
+    )
+
+
+def finish_kernel(blocks, points, parts, core, mine, other, turn_re, turn_im, kept, *refs):
+    spectra_refs = [(refs[2 * n], refs[2 * n + 1]) for n in range(parts)]
+    energy, modes, tiles, basis = refs[2 * parts :]
+    step = pl.program_id(0)
+
+    @pl.when(step == 0)
+    def _():
+        swap = core[0] == 1
+        half = mine.shape[1]
+        count = 2 * half // LANES
+        for t in range(count):
+            lane = slice(t * LANES % half, t * LANES % half + LANES)
+            ours = jnp.logical_xor(swap, t * LANES >= half)
+            tiles[t] = jnp.where(ours, other[:, lane], mine[:, lane]) * (1.0 / points)
+        ph = (turn_re[...], turn_im[...])
+        back = (ph[0], -ph[1])
+        row = lax.broadcasted_iota(jnp.int32, ph[0].shape, 0)
+        g = []
+        for e in range(blocks):
+            down = [tiles[t, e * blocks : (e + 1) * blocks, :] for t in range(count)]
+            across = [tiles[t, pl.ds(e, blocks, stride=blocks), :] for t in range(count)]
+            down, across = jnp.concatenate(down, axis=1), jnp.concatenate(across, axis=1)
+            re = jnp.where(row <= e, down, across)
+            im = jnp.where(row < e, across, jnp.where(row > e, -down, 0.0))
+            column = (ph[0][e : e + 1], ph[1][e : e + 1])
+            g.append(cmul(cmul(back, (re, im)), column))
+        ys = g[:MODES]
+        for sweep in range(ITERS):
+            done = []
+            for v in ys:
+                for q in done:
+                    part = cmul(row_dot(q, v), q)
+                    v = (v[0] - part[0], v[1] - part[1])
+                length = jnp.sqrt(jnp.sum(v[0] * v[0] + v[1] * v[1], axis=0, keepdims=True))
+                done.append((v[0] / length, v[1] / length))
+            ys = []
+            for q in done:
+                re, im = jnp.zeros_like(q[0]), jnp.zeros_like(q[0])
+                for e in range(blocks):
+                    part = cmul(g[e], (q[0][e : e + 1], q[1][e : e + 1]))
+                    re, im = re + part[0], im + part[1]
+                ys.append((re, im))
+        for m, (q, y) in enumerate(zip(done, ys)):
+            level = row_dot(q, y)[0]
+            energy[m : m + 1, :] = level
+            factor = jnp.where(kept[...] > m, 1.0, 0.0) / jnp.sqrt(level)
+            re, im = cmul(ph, q)
+            re, im = re * factor, im * factor
+            for t in range(count):
+                lane = slice(t * LANES, (t + 1) * LANES)
+                basis[t, 2 * m * blocks : (2 * m + 1) * blocks, :] = re[:, lane]
+                basis[t, (2 * m + 1) * blocks : (2 * m + 2) * blocks, :] = im[:, lane]
+
+    where = []
+    for re, im in spectra_refs:
+        where += [(re, im, n * LANES) for n in range(re.shape[0] // LANES)]
+    for m in range(MODES):
+        total_re, total_im = None, None
+        for b, (re, im, base) in enumerate(where):
+            u = (re[base : base + LANES, :], im[base : base + LANES, :])
+            q = [basis[step, pl.ds((2 * m + n) * blocks + b, 1), :] for n in (0, 1)]
+            part = cmul(u, q)
+            total_re = part[0] if b == 0 else total_re + part[0]
+            total_im = part[1] if b == 0 else total_im + part[1]
+        modes[m, 0] = total_re
+        modes[m, 1] = total_im
+
+
+def finish(blocks, points, core, mine, other, turn, kept, parts):
+    square, half = mine.shape
+    bins = 2 * half
+    flat = [a for part in parts for a in part]
+    whole = lambda a: pl.BlockSpec(a.shape, lambda i, c: (0, 0))
+    kept = kept.reshape(1, bins)
+    small = [mine, other, *turn, kept]
+    return pl.pallas_call(
+        lambda *refs: finish_kernel(blocks, points, len(parts), *refs),
+        grid_spec=pltpu.PrefetchScalarGridSpec(
+            num_scalar_prefetch=1,
+            grid=(bins // LANES,),
+            in_specs=[whole(a) for a in small]
+            + [pl.BlockSpec((a.shape[0], LANES), lambda i, c: (0, i)) for a in flat],
+            out_specs=[
+                pl.BlockSpec((MODES, bins), lambda i, c: (0, 0)),
+                pl.BlockSpec((MODES, 2, LANES, LANES), lambda i, c: (0, 0, 0, i)),
+            ],
+            scratch_shapes=[
+                pltpu.VMEM((bins // LANES, square, LANES), jnp.float32),
+                pltpu.VMEM((bins // LANES, 2 * MODES * blocks, LANES), jnp.float32),
+            ],
+        ),
+        out_shape=[
+            jax.ShapeDtypeStruct((MODES, bins), jnp.float32),
+            jax.ShapeDtypeStruct((MODES, 2, LANES, bins), jnp.float32),
+        ],
+        compiler_params=SMALL,
+        cost_estimate=pl.CostEstimate(
+            flops=16 * MODES * blocks * LANES * bins, bytes_accessed=6 * 2**20, transcendentals=0
+        ),
+    )(core, *small, *flat)
+
+
+def gram_of(u, blocks):
+    pairs = []
+    for b, e in pair_list(blocks):
+        pairs.append(jnp.sum(u[0][b] * u[0][e] + u[1][b] * u[1][e], axis=0))
+        if e > b:
+            pairs.append(jnp.sum(u[0][b] * u[1][e] - u[1][b] * u[0][e], axis=0))
+    return jnp.stack(pairs, axis=0)
+
+
+def plain(signal, offsets, pairing, modes_kept):
     rows, blocks, points = signal.shape
     ranks = lax.axis_size("freq")
     rank = lax.axis_index("freq")
@@ -86,13 +416,7 @@
     spectra = lax.dot_general(series, table, (((0,), (0,)), ((), ())), precision=precise)
     spectra = spectra.reshape(blocks, own, 2, bins)
     u = (spectra[:, :, 0], spectra[:, :, 1])
-    pairs = []
-    for b in range(blocks):
-        for e in range(b, blocks):
-            pairs.append(jnp.sum(u[0][b] * u[0][e] + u[1][b] * u[1][e], axis=0))
-            if e > b:
-                pairs.append(jnp.sum(u[0][b] * u[1][e] - u[1][b] * u[0][e], axis=0))
-    sums = sum_over(jnp.stack(pairs, axis=0), "freq") * (1.0 / points)
+    sums = sum_over(gram_of(u, blocks), "freq") * (1.0 / points)
     g_re = [[None] * blocks for _ in range(blocks)]
     g_im = [[None] * blocks for _ in range(blocks)]
     at = 0
@@ -121,7 +445,56 @@
         re = jnp.sum(u[0] * q[0][:, None] - u[1] * q[1][:, None], axis=0)
         im = jnp.sum(u[0] * q[1][:, None] + u[1] * q[0][:, None], axis=0)
         modes.append(jnp.stack([re, im]))
-    modes = jnp.stack(modes).reshape(MODES, 2, 2, own // 2, bins)
+    return energy, jnp.stack(modes)
+
+
+CHUNKS = (4, 4)
+
+
+def swap_with(values, step):
+    ranks = lax.axis_size("freq")
+    return lax.ppermute(values, "freq", [(i, i ^ step) for i in range(ranks)])
+
+
+def tiled(signal, offsets, pairing, modes_kept):
+    rows, blocks, points = signal.shape
+    ranks = lax.axis_size("freq")
+    rank = lax.axis_index("freq")
+    bins = rows * ranks // 2
+    core = (rank & 1).reshape(1)
+    turn = phase_table(offsets, bins, rows * ranks)
+    tables = [jnp.asarray(t) for t in split_table(rows * ranks)]
+    got, first = [], 0
+    for count in CHUNKS:
+        part = pack(signal, pairing, first, count)
+        signal, part = lax.optimization_barrier((signal, part))
+        got.append(lax.all_to_all(part, "freq", split_axis=0, concat_axis=0, tiled=True))
+        first += count
+    parts, gram = [], None
+    for n, x in enumerate(got):
+        final = n == len(got) - 1
+        re, im, *grams = spectra(blocks, x.reshape(rows * ranks, -1), tables, core, parts, gram, final)
+        parts.append((re, im))
+        gram = grams[0]
+    mine = gram + swap_with(grams[1], 1)
+    step = 2
+    while step < ranks:
+        mine = mine + swap_with(mine, step)
+        step *= 2
+    other = swap_with(mine, 1)
+    energy, modes = finish(blocks, points, core, mine, other, turn, modes_kept, parts)
+    return energy, modes
+
+
+def local(signal, offsets, pairing, modes_kept):
+    rows, blocks, points = signal.shape
+    ranks = lax.axis_size("freq")
+    rank = lax.axis_index("freq")
+    bins = rows * ranks // 2
+    fits = points == ranks * LANES and rows % 16 == 0 and ranks >= GROUP and ranks & (ranks - 1) == 0
+    fits = fits and bins % (2 * LANES) == 0 and blocks == sum(CHUNKS) == 8
+    energy, modes = (tiled if fits else plain)(signal, offsets, pairing, modes_kept)
+    modes = modes.reshape(MODES, 2, 2, points // ranks // 2, bins)
     held = lax.dynamic_slice_in_dim(energy, rank * (bins // ranks), bins // ranks, axis=1)
     return held.T, modes.transpose(4, 0, 1, 2, 3)
 

time: 197 us -> 162 us (0.82)
  blocking collectives: 99.4 us -> 0 us
  waiting for transfers between devices: 13.9 us -> 68.3 us
  Pallas kernels: 0 us -> 41.7 us
  local copies, waits for them, and re-layouts: 45.2 us -> 17.7 us
  starting transfers between devices: 6.61 us -> 32.2 us
  matrix products: 17 us -> 0 us
  other arithmetic: 13.2 us -> 0.19 us
    all_to_all x1 -> x0, blocking collectives: 99.4 us -> none  [local(): lax.all_to_all(packed, 'freq', split_axis=0, concat_axis=0, tiled=True)]
    all_to_all x0 -> x2, waiting for transfers between devices: none -> 59.2 us  [tiled(): lax.all_to_all(part, 'freq', split_axis=0, concat_axis=0, tiled=True)]
    pallas_call x0 -> x5, Pallas kernels: none -> 41.7 us  [the longest x2 21.4 us: pack(): pl.pallas_call(lambda *refs: pack_kernel(blocks, first, count, strips, *r...]
    gather x2 -> x0, local copies, waits for them, and re-layouts: 26 us -> none  [local(): packed = jnp.take(signal, order, axis=2).reshape(rows, blocks, ranks, own)]
    all_to_all x0 -> x2, starting transfers between devices: none -> 18.6 us  [tiled(): lax.all_to_all(part, 'freq', split_axis=0, concat_axis=0, tiled=True)]
    dot_general x1 -> x0, matrix products: 17 us -> none  [local(): lax.dot_general(series, table, (((0,), (0,)), ((), ())), precision=precise)]
    reduce_sum x40 -> x0, other arithmetic: 8.56 us -> none  [the longest x1 2.65 us: local(): re = jnp.sum(u[0] * q[0][:, None] - u[1] * q[1][:, None], axis=0)]
    ppermute x4 -> x5, starting transfers between devices: 6.61 us -> 13.7 us  [swap_with(): return lax.ppermute(values, 'freq', [(i, i ^ step) for i in range(ranks)])]
  transfers between devices with their start and end apart: 4 -> 7, of which waited for: 4 -> 7; matrix products, arithmetic and copies ran while one was open for 0% -> 0% of each run, Pallas kernels for 0% -> 11%
where the time goes in v3:
time: 162 us; the launch traced here: 161 us
  waiting for transfers between devices  68.3 us (42%)
  Pallas kernels  41.7 us (26%)
  starting transfers between devices  32.2 us (20%)
  local copies, waits for them, and re-layouts  17.7 us (11%)
    all_to_all x2, waiting for transfers between devices, tiled(): lax.all_to_all(part, 'freq', split_axis=0, concat_axis=0, tiled=True)  59.2 us
    pallas_call x2, Pallas kernels, pack(): pl.pallas_call(lambda *refs: pack_kernel(blocks, first, count, strips, *r...  21.4 us
    all_to_all x2, starting transfers between devices, tiled(): lax.all_to_all(part, 'freq', split_axis=0, concat_axis=0, tiled=True)  18.6 us
    unnamed x30, local copies, waits for them, and re-layouts  17.1 us
    pallas_call x2, Pallas kernels, spectra(): pl.pallas_call(lambda *refs: spectra_kernel(blocks, len(others), final, *...  15.4 us
    ppermute x5, starting transfers between devices, swap_with(): return lax.ppermute(values, 'freq', [(i, i ^ step) for i in range(ranks)])  13.7 us
    ppermute x5, waiting for transfers between devices, swap_with(): return lax.ppermute(values, 'freq', [(i, i ^ step) for i in range(ranks)])  9.08 us
    pallas_call x1, Pallas kernels, finish(): pl.pallas_call(lambda *refs: finish_kernel(blocks, points, len(parts), *r...  4.85 us
  transfers between devices with their start and end apart: 7, of which 7 were waited for; matrix products, arithmetic and copies ran while one was open for 0% of the time, Pallas kernels for 11%

profile of v3, /device:TPU:0, one launch (start us, length us, event | category | flops | bytes accessed | tf_op | source)
XLA Modules:
  0.0 160.9 jit_solution(14603413814190098246)
XLA Ops:
  0.6 10.7 %shard_map.77 = f32[16,64,512]{2,1,0:T(8,128)} custom-call(f32[512,2048]{1,0:T(8,128)} %bitcast.15, f32[512,2048]{1,0:T(8,128)} %bitcast.16, f32[512,2048]{1,0:T(8,128)} %bitcast.17, f32[512,2048]{1,0:T(8,128)} %bitcast.18, s32[16,128]{1,0:T(8,128)} %bitcast.24), custom_call_target="tpu_custom_call" | custom-call | flops 6442450944 | bytes 8388608 | tf_op jit(solution)/shard_map/pallas_call | solution.py:160
  11.3 7.4 %all-to-all-start.1 = ((f32[16,64,512]{2,1,0:T(8,128)}), f32[16,64,512]{2,1,0:T(8,128)S(1)}, u32[]{:S(2)}, u32[]{:S(2)}) async-start(f32[16,64,512]{2,1,0:T(8,128)} %shard_map.77), calls=%async_computation.1 | async-start | bytes 4194304 | tf_op jit(solution)/shard_map/all_to_all | solution.py:471
  18.7 10.7 %shard_map.78 = f32[16,64,512]{2,1,0:T(8,128)} custom-call(f32[512,2048]{1,0:T(8,128)} %bitcast.19, f32[512,2048]{1,0:T(8,128)} %bitcast.20, f32[512,2048]{1,0:T(8,128)} %bitcast.21, f32[512,2048]{1,0:T(8,128)} %bitcast.22, s32[16,128]{1,0:T(8,128)} %bitcast.25), custom_call_target="tpu_custom_call" | custom-call | flops 6442450944 | bytes 8388608 | tf_op jit(solution)/shard_map/pallas_call | solution.py:160
  29.4 30.4 %all-to-all-done.1 = f32[16,64,512]{2,1,0:T(8,128)S(1)} async-done(((f32[16,64,512]{2,1,0:T(8,128)}), f32[16,64,512]{2,1,0:T(8,128)S(1)}, u32[]{:S(2)}, u32[]{:S(2)}) %all-to-all-start.1) | async-done | bytes 2097184 | tf_op jit(solution)/shard_map/all_to_all | solution.py:471
  59.8 1.3 copy-done
  61.1 11.2 %all-to-all-start = ((f32[16,64,512]{2,1,0:T(8,128)}), f32[16,64,512]{2,1,0:T(8,128)S(1)}, u32[]{:S(2)}, u32[]{:S(2)}) async-start(f32[16,64,512]{2,1,0:T(8,128)} %shard_map.78), calls=%async_computation | async-start | bytes 4194304 | tf_op jit(solution)/shard_map/all_to_all | solution.py:471
  72.4 1.6 copy-done.1
  74.0 1.6 copy-done.10
  75.5 1.6 copy-done.12
  77.1 6.5 %shard_map.79 = (f32[512,512]{1,0:T(8,128)S(1)}, f32[512,512]{1,0:T(8,128)S(1)}, f32[64,512]{1,0:T(8,128)S(1)}) custom-call(s32[1]{0:T(128)} %bitcast.refs_0_, f32[1024,512]{1,0:T(8,128)S(1)} %bitcast.13, bf16[1024,1024]{1,0:T(8,128)(2,1)S(1)} %copy-done.10, bf16[1024,1024]{1,0:T(8,128)(2,1)S(1)} %copy-done.12), custom_call_target="tpu_custom_call" | custom-call | flops 3221225472 | bytes 12582912 | tf_op jit(solution)/shard_map/pallas_call | solution.py:267
  84.6 28.8 %all-to-all-done = f32[16,64,512]{2,1,0:T(8,128)S(1)} async-done(((f32[16,64,512]{2,1,0:T(8,128)}), f32[16,64,512]{2,1,0:T(8,128)S(1)}, u32[]{:S(2)}, u32[]{:S(2)}) %all-to-all-start) | async-done | bytes 2097184 | tf_op jit(solution)/shard_map/all_to_all | solution.py:471
  113.5 1.2 copy-done.3
  114.7 1.6 copy-done.11
  116.3 1.6 copy-done.13
  117.9 9.0 %shard_map.80 = (f32[512,512]{1,0:T(8,128)S(1)}, f32[512,512]{1,0:T(8,128)S(1)}, f32[64,256]{1,0:T(8,128)S(1)}, f32[64,256]{1,0:T(8,128)S(1)}) custom-call(s32[1]{0:T(128)} %bitcast.refs_0_, f32[1024,512]{1,0:T(8,128)S(1)} %bitcast.12, bf16[1024,1024]{1,0:T(8,128)(2,1)S(1)} %copy-done.11, bf16[1024,1024]{1,0:T(8,128)(2,1)S(1)} %copy-done.13, ...), custom_call_target="tpu_custom_call" | custom-call | flops 3221225472 | bytes 12582912 | tf_op jit(solution)/shard_map/pallas_call | solution.py:267
  130.5 3.4 %collective-permute-start.1 = (f32[64,256]{1,0:T(8,128)S(1)}, f32[64,256]{1,0:T(8,128)S(1)}, u32[]{:S(2)}, u32[]{:S(2)}) collective-permute-start(f32[64,256]{1,0:T(8,128)S(1)} %add.21), channel_id=1, source_target_pairs={{0,2},{1,3},{2,0},{3,1},{4,6},{5,7},{6,4},{7,5},{8,10},{9,11},{10,... | collective-permute-start | bytes 196616 | tf_op jit(solution)/shard_map/ppermute | solution.py:456
  133.9 2.6 %collective-permute-done.1 = f32[64,256]{1,0:T(8,128)S(1)} collective-permute-done((f32[64,256]{1,0:T(8,128)S(1)}, f32[64,256]{1,0:T(8,128)S(1)}, u32[]{:S(2)}, u32[]{:S(2)}) %collective-permute-start.1) | collective-permute-done | bytes 65568 | tf_op jit(solution)/shard_map/ppermute | solution.py:456
  136.5 5.8 %collective-permute-start.2 = (f32[64,256]{1,0:T(8,128)S(1)}, f32[64,256]{1,0:T(8,128)S(1)}, u32[]{:S(2)}, u32[]{:S(2)}) collective-permute-start(f32[64,256]{1,0:T(8,128)S(1)} %add.22), channel_id=1, source_target_pairs={{0,4},{1,5},{2,6},{3,7},{4,0},{5,1},{6,2},{7,3},{8,12},{9,13},{10,... | collective-permute-start | bytes 196616 | tf_op jit(solution)/shard_map/ppermute | solution.py:456
  142.3 2.2 %collective-permute-done.2 = f32[64,256]{1,0:T(8,128)S(1)} collective-permute-done((f32[64,256]{1,0:T(8,128)S(1)}, f32[64,256]{1,0:T(8,128)S(1)}, u32[]{:S(2)}, u32[]{:S(2)}) %collective-permute-start.2) | collective-permute-done | bytes 65568 | tf_op jit(solution)/shard_map/ppermute | solution.py:456
  144.6 3.6 %collective-permute-start.3 = (f32[64,256]{1,0:T(8,128)S(1)}, f32[64,256]{1,0:T(8,128)S(1)}, u32[]{:S(2)}, u32[]{:S(2)}) collective-permute-start(f32[64,256]{1,0:T(8,128)S(1)} %add.23), channel_id=1, source_target_pairs={{0,8},{1,9},{2,10},{3,11},{4,12},{5,13},{6,14},{7,15},{8,0},{9,1},... | collective-permute-start | bytes 196616 | tf_op jit(solution)/shard_map/ppermute | solution.py:456
  148.2 2.2 %collective-permute-done.3 = f32[64,256]{1,0:T(8,128)S(1)} collective-permute-done((f32[64,256]{1,0:T(8,128)S(1)}, f32[64,256]{1,0:T(8,128)S(1)}, u32[]{:S(2)}, u32[]{:S(2)}) %collective-permute-start.3) | collective-permute-done | bytes 65568 | tf_op jit(solution)/shard_map/ppermute | solution.py:456
  151.7 1.2 copy-done.4
  153.0 1.2 copy-done.6
  155.4 4.8 %shard_map.81 = (f32[4,512]{1,0:T(4,128)S(1)}, f32[4,2,128,512]{3,2,1,0:T(8,128)}) custom-call(s32[1]{0:T(128)} %bitcast.refs_0_, f32[64,256]{1,0:T(8,128)S(1)} %add.24.refs_1_, f32[64,256]{1,0:T(8,128)S(1)} %collective-permute-done.4.refs_2_, f32[8,512]{1,0:T(8,128)S(1)} %get-tuple-element.27.refs_3_, f32[8,512]{1,0:T(8,128)S(1)} %get-tuple-element.26.refs_4_, ...), custom_call_target="tpu_custom_call" | custom-call | flops 33554432 | bytes 6291456 | tf_op jit(solution)/shard_map/pallas_call | solution.py:367
  (31 shorter events, 7.8 us)
Async XLA Ops:
  11.3 48.5 %all-to-all-start.1 = ((f32[16,64,512]{2,1,0:T(8,128)}), f32[16,64,512]{2,1,0:T(8,128)S(1)}, u32[]{:S(2)}, u32[]{:S(2)}) async-start(f32[16,64,512]{2,1,0:T(8,128)} %shard_map.77), calls=%async_computation.1 | async-start | bytes 4194304 | tf_op jit(solution)/shard_map/all_to_all | solution.py:471
  59.8 1.3 copy-start
  61.1 52.3 %all-to-all-start = ((f32[16,64,512]{2,1,0:T(8,128)}), f32[16,64,512]{2,1,0:T(8,128)S(1)}, u32[]{:S(2)}, u32[]{:S(2)}) async-start(f32[16,64,512]{2,1,0:T(8,128)} %shard_map.78), calls=%async_computation | async-start | bytes 4194304 | tf_op jit(solution)/shard_map/all_to_all | solution.py:471
  72.4 1.6 copy-start.1
  74.0 1.6 copy-start.10
  75.5 1.6 copy-start.12
  83.6 1.0 copy-start.2
  113.5 1.2 copy-start.3
  114.7 1.6 copy-start.11
  116.3 1.6 copy-start.13
  117.9 32.6 %copy-start.14 = (s32[8]{0:T(128)S(1)}, s32[8]{0:T(128)}, u32[]{:S(2)}) copy-start(s32[8]{0:T(128)} %param.7) | copy-start | bytes 100
  117.9 33.9 %copy-start.9 = (s32[512]{0:T(512)S(1)}, s32[512]{0:T(512)}, u32[]{:S(2)}) copy-start(s32[512]{0:T(512)} %param.9) | copy-start | bytes 6148
  126.8 1.0 copy-start.5
  127.8 0.9 copy-start.7
  128.8 1.7 %collective-permute-start = (f32[64,256]{1,0:T(8,128)S(1)}, f32[64,256]{1,0:T(8,128)S(1)}, u32[]{:S(2)}, u32[]{:S(2)}) collective-permute-start(f32[64,256]{1,0:T(8,128)S(1)} %get-tuple-element.21), channel_id=1, source_target_pairs={{0,1},{1,0},{2,3},{3,2},{4,5},{5,4},{6,7},{7,6},{8,9},{9,8},{10,11... | collective-permute-start | bytes 196616 | tf_op jit(solution)/shard_map/ppermute | solution.py:456
  130.5 6.0 %collective-permute-start.1 = (f32[64,256]{1,0:T(8,128)S(1)}, f32[64,256]{1,0:T(8,128)S(1)}, u32[]{:S(2)}, u32[]{:S(2)}) collective-permute-start(f32[64,256]{1,0:T(8,128)S(1)} %add.21), channel_id=1, source_target_pairs={{0,2},{1,3},{2,0},{3,1},{4,6},{5,7},{6,4},{7,5},{8,10},{9,11},{10,... | collective-permute-start | bytes 196616 | tf_op jit(solution)/shard_map/ppermute | solution.py:456
  136.5 8.0 %collective-permute-start.2 = (f32[64,256]{1,0:T(8,128)S(1)}, f32[64,256]{1,0:T(8,128)S(1)}, u32[]{:S(2)}, u32[]{:S(2)}) collective-permute-start(f32[64,256]{1,0:T(8,128)S(1)} %add.22), channel_id=1, source_target_pairs={{0,4},{1,5},{2,6},{3,7},{4,0},{5,1},{6,2},{7,3},{8,12},{9,13},{10,... | collective-permute-start | bytes 196616 | tf_op jit(solution)/shard_map/ppermute | solution.py:456
  144.6 5.9 %collective-permute-start.3 = (f32[64,256]{1,0:T(8,128)S(1)}, f32[64,256]{1,0:T(8,128)S(1)}, u32[]{:S(2)}, u32[]{:S(2)}) collective-permute-start(f32[64,256]{1,0:T(8,128)S(1)} %add.23), channel_id=1, source_target_pairs={{0,8},{1,9},{2,10},{3,11},{4,12},{5,13},{6,14},{7,15},{8,0},{9,1},... | collective-permute-start | bytes 196616 | tf_op jit(solution)/shard_map/ppermute | solution.py:456
  150.4 1.3 collective-permute-start.4
  151.7 1.2 copy-start.4
  153.0 1.2 copy-start.6
  154.2 1.2 copy-start.8

commit v4 on v3

--- a/solution.py
+++ b/solution.py
@@ -76,7 +76,7 @@
 LANES = 128
 GROUP = 4
 VMEM = pltpu.CompilerParams(vmem_limit_bytes=60 * 2**20)
-SMALL = pltpu.CompilerParams(vmem_limit_bytes=32 * 2**20)
+SMALL = pltpu.CompilerParams(vmem_limit_bytes=50 * 2**20)
 
 
 def split_table(frames):
@@ -103,8 +103,12 @@
     return jnp.dot(a, b, preferred_element_type=jnp.float32)
 
 
+def in_hbm(arrays):
+    return [pltpu.with_memory_space_constraint(a, pltpu.HBM) for a in arrays]
+
+
 def pack_kernel(blocks, first, count, strips, *refs):
-    signals, pairing, out, one_row, total = refs[:strips], *refs[strips:]
+    signals, pairing, out, one_row, low_pick, total = refs[:strips], *refs[strips:]
     step = pl.program_id(0)
     rows = signals[0].shape[0] // blocks
     ranks = out.shape[0]
@@ -122,6 +126,10 @@
         lower = (lines & 31).astype(jnp.float32).astype(jnp.bfloat16)
         one_row[...] = (dot(upper, turn) * 32.0 + dot(lower, turn)).astype(jnp.int32)
         total[...] = jnp.zeros_like(total)
+        for n in range(ranks):
+            low_pick[:, n * LANES : (n + 1) * LANES] = jnp.where(
+                source == one_row[n : n + 1, :] % LANES, 1.0, 0.0
+            ).astype(jnp.bfloat16)
 
     x = jnp.concatenate(
         [
@@ -130,18 +138,22 @@
         ],
         axis=0,
     )
-    terms = three_terms(x)
-    source = lax.broadcasted_iota(jnp.int32, (depth, LANES), 0) + step * depth
+    stacked = jnp.concatenate(three_terms(x), axis=0)
+    third = stacked.shape[0] // 3
+    here = [
+        jnp.where(one_row[...] // LANES == step * strips + n, 1.0, 0.0) for n in range(strips)
+    ]
     for at in range(0, ranks, GROUP):
-        pick = jnp.concatenate(
-            [
-                jnp.where(source == one_row[n : n + 1, :], 1.0, 0.0).astype(jnp.bfloat16)
-                for n in range(at, at + GROUP)
-            ],
-            axis=1,
-        )
+        pick = []
+        for n in range(at, at + GROUP):
+            spot = low_pick[:, n * LANES : (n + 1) * LANES]
+            strip = [
+                spot * jnp.broadcast_to(line[n : n + 1], spot.shape).astype(jnp.bfloat16) for line in here
+            ]
+            pick.append(jnp.concatenate(strip, axis=0))
+        got = dot(stacked, jnp.concatenate(pick, axis=1))
         spot = (slice(None), slice(at * LANES, (at + GROUP) * LANES))
-        total[spot] += dot(terms[0], pick) + dot(terms[1], pick) + dot(terms[2], pick)
+        total[spot] += got[:third] + got[third : 2 * third] + got[2 * third :]
 
     @pl.when(step == pl.num_programs(0) - 1)
     def _():
@@ -168,6 +180,7 @@
         out_specs=pl.BlockSpec(shape, lambda i: (0, 0, 0)),
         scratch_shapes=[
             pltpu.VMEM((ranks, LANES), jnp.int32),
+            pltpu.VMEM((LANES, points), jnp.bfloat16),
             pltpu.VMEM((rows * count, points), jnp.float32),
         ],
         out_shape=jax.ShapeDtypeStruct(shape, jnp.float32),
@@ -252,7 +265,7 @@
     frames, width = x.shape
     bins = frames // 2
     held = pl.BlockSpec((width, LANES), lambda i, c: (0, i))
-    shape = jax.ShapeDtypeStruct((width, bins), jnp.float32)
+    shape = pltpu.HBM((width, bins), jnp.float32)
     flat = [a for part in others for a in part] + ([before] if others else [])
     in_specs = [pl.BlockSpec((frames, width), lambda i, c: (0, 0))]
     in_specs += [pl.BlockSpec((frames, 2 * LANES), lambda i, c: (0, i))] * 2
@@ -279,7 +292,7 @@
         cost_estimate=pl.CostEstimate(
             flops=6 * width * frames * frames, bytes_accessed=12 * 2**20, transcendentals=0
         ),
-    )(core, x, *tables, *flat)
+    )(core, x, *in_hbm([*tables, *flat]))
 
 
 def row_dot(a, b):
@@ -388,7 +401,7 @@
         cost_estimate=pl.CostEstimate(
             flops=16 * MODES * blocks * LANES * bins, bytes_accessed=6 * 2**20, transcendentals=0
         ),
-    )(core, *small, *flat)
+    )(core, *small, *in_hbm(flat))
 
 
 def gram_of(u, blocks):

time: 162 us -> 154 us (0.951)
  local copies, waits for them, and re-layouts: 17.7 us -> 4.23 us
  Pallas kernels: 41.7 us -> 45.5 us
  waiting for transfers between devices: 68.3 us -> 70.5 us
    unnamed x30 -> x10, local copies, waits for them, and re-layouts: 17.1 us -> 3.58 us
    pallas_call x2, Pallas kernels: 15.4 us -> 18.1 us  [spectra(): pl.pallas_call(lambda *refs: spectra_kernel(blocks, len(others), final, *...]
    all_to_all x2, waiting for transfers between devices: 59.2 us -> 61.5 us  [tiled(): lax.all_to_all(part, 'freq', split_axis=0, concat_axis=0, tiled=True)]
  transfers between devices with their start and end apart: 7 -> 7, of which waited for: 7 -> 7; matrix products, arithmetic and copies ran while one was open for 0% -> 0% of each run, Pallas kernels for 11% -> 12%
where the time goes in v4:
time: 154 us; the launch traced here: 153 us
  waiting for transfers between devices  70.5 us (46%)
  Pallas kernels  45.5 us (30%)
  starting transfers between devices  32.2 us (21%)
  local copies, waits for them, and re-layouts  4.23 us (3%)
    all_to_all x2, waiting for transfers between devices, tiled(): lax.all_to_all(part, 'freq', split_axis=0, concat_axis=0, tiled=True)  61.5 us
    pallas_call x2, Pallas kernels, pack(): pl.pallas_call(lambda *refs: pack_kernel(blocks, first, count, strips, *r...  21.2 us
    all_to_all x2, starting transfers between devices, tiled(): lax.all_to_all(part, 'freq', split_axis=0, concat_axis=0, tiled=True)  18.6 us
    pallas_call x2, Pallas kernels, spectra(): pl.pallas_call(lambda *refs: spectra_kernel(blocks, len(others), final, *...  18.1 us
    ppermute x5, starting transfers between devices, swap_with(): return lax.ppermute(values, 'freq', [(i, i ^ step) for i in range(ranks)])  13.7 us
    ppermute x5, waiting for transfers between devices, swap_with(): return lax.ppermute(values, 'freq', [(i, i ^ step) for i in range(ranks)])  9.08 us
    pallas_call x1, Pallas kernels, finish(): pl.pallas_call(lambda *refs: finish_kernel(blocks, points, len(parts), *r...  6.26 us
    unnamed x10, local copies, waits for them, and re-layouts  3.58 us
  transfers between devices with their start and end apart: 7, of which 7 were waited for; matrix products, arithmetic and copies ran while one was open for 0% of the time, Pallas kernels for 12%

profile of v4, /device:TPU:0, one launch (start us, length us, event | category | flops | bytes accessed | tf_op | source)
XLA Modules:
  0.0 153.4 jit_solution(10028269911224462275)
XLA Ops:
  0.6 10.6 %shard_map.77 = f32[16,64,512]{2,1,0:T(8,128)} custom-call(f32[512,2048]{1,0:T(8,128)} %bitcast.15, f32[512,2048]{1,0:T(8,128)} %bitcast.16, f32[512,2048]{1,0:T(8,128)} %bitcast.17, f32[512,2048]{1,0:T(8,128)} %bitcast.18, s32[16,128]{1,0:T(8,128)} %bitcast.24), custom_call_target="tpu_custom_call" | custom-call | flops 6442450944 | bytes 8388608 | tf_op jit(solution)/shard_map/pallas_call | solution.py:172
  11.2 7.4 %all-to-all-start.1 = ((f32[16,64,512]{2,1,0:T(8,128)}), f32[16,64,512]{2,1,0:T(8,128)S(1)}, u32[]{:S(2)}, u32[]{:S(2)}) async-start(f32[16,64,512]{2,1,0:T(8,128)} %shard_map.77), calls=%async_computation.1 | async-start | bytes 4194304 | tf_op jit(solution)/shard_map/all_to_all | solution.py:484
  18.6 10.6 %shard_map.78 = f32[16,64,512]{2,1,0:T(8,128)} custom-call(f32[512,2048]{1,0:T(8,128)} %bitcast.19, f32[512,2048]{1,0:T(8,128)} %bitcast.20, f32[512,2048]{1,0:T(8,128)} %bitcast.21, f32[512,2048]{1,0:T(8,128)} %bitcast.22, s32[16,128]{1,0:T(8,128)} %bitcast.25), custom_call_target="tpu_custom_call" | custom-call | flops 6442450944 | bytes 8388608 | tf_op jit(solution)/shard_map/pallas_call | solution.py:172
  29.2 30.5 %all-to-all-done.1 = f32[16,64,512]{2,1,0:T(8,128)S(1)} async-done(((f32[16,64,512]{2,1,0:T(8,128)}), f32[16,64,512]{2,1,0:T(8,128)S(1)}, u32[]{:S(2)}, u32[]{:S(2)}) %all-to-all-start.1) | async-done | bytes 2097184 | tf_op jit(solution)/shard_map/all_to_all | solution.py:484
  59.7 1.3 copy-done
  61.0 11.2 %all-to-all-start = ((f32[16,64,512]{2,1,0:T(8,128)}), f32[16,64,512]{2,1,0:T(8,128)S(1)}, u32[]{:S(2)}, u32[]{:S(2)}) async-start(f32[16,64,512]{2,1,0:T(8,128)} %shard_map.78), calls=%async_computation | async-start | bytes 4194304 | tf_op jit(solution)/shard_map/all_to_all | solution.py:484
  72.3 1.6 %copy-done.1 = f32[16,64,512]{2,1,0:T(8,128)S(1)} copy-done((f32[16,64,512]{2,1,0:T(8,128)S(1)}, f32[16,64,512]{2,1,0:T(8,128)}, u32[]{:S(2)}) %copy-start.1) | copy-done | bytes 2097176
  73.9 7.9 %shard_map.79 = (f32[512,512]{1,0:T(8,128)}, f32[512,512]{1,0:T(8,128)}, f32[64,512]{1,0:T(8,128)S(1)}) custom-call(s32[1]{0:T(128)} %bitcast.refs_0_, f32[1024,512]{1,0:T(8,128)S(1)} %bitcast.13, bf16[1024,1024]{1,0:T(8,128)(2,1)} %constant.32.clone.refs_2_, bf16[1024,1024]{1,0:T(8,128)(2,1)} %constant.33.clone.refs_3_), custom_call_target="tpu_custom_call" | custom-call | flops 3221225472 | bytes 12582912 | tf_op jit(solution)/shard_map/pallas_call | solution.py:280
  81.8 0.6 copy-done.3
  82.4 30.9 %all-to-all-done = f32[16,64,512]{2,1,0:T(8,128)S(1)} async-done(((f32[16,64,512]{2,1,0:T(8,128)}), f32[16,64,512]{2,1,0:T(8,128)S(1)}, u32[]{:S(2)}, u32[]{:S(2)}) %all-to-all-start) | async-done | bytes 2097184 | tf_op jit(solution)/shard_map/all_to_all | solution.py:484
  113.4 10.1 %shard_map.80 = (f32[512,512]{1,0:T(8,128)}, f32[512,512]{1,0:T(8,128)}, f32[64,256]{1,0:T(8,128)S(1)}, f32[64,256]{1,0:T(8,128)S(1)}) custom-call(s32[1]{0:T(128)} %bitcast.refs_0_, f32[1024,512]{1,0:T(8,128)S(1)} %bitcast.12, bf16[1024,1024]{1,0:T(8,128)(2,1)} %constant.32.clone.refs_2_, bf16[1024,1024]{1,0:T(8,128)(2,1)} %constant.33.clone.refs_3_, ...), custom_call_target="tpu_custom_call" | custom-call | flops 3221225472 | bytes 12582912 | tf_op jit(solution)/shard_map/pallas_call | solution.py:280
  123.5 0.8 collective-permute-start
  124.3 0.9 collective-permute-done
  125.2 3.4 %collective-permute-start.1 = (f32[64,256]{1,0:T(8,128)S(1)}, f32[64,256]{1,0:T(8,128)S(1)}, u32[]{:S(2)}, u32[]{:S(2)}) collective-permute-start(f32[64,256]{1,0:T(8,128)S(1)} %add.21), channel_id=1, source_target_pairs={{0,2},{1,3},{2,0},{3,1},{4,6},{5,7},{6,4},{7,5},{8,10},{9,11},{10,... | collective-permute-start | bytes 196616 | tf_op jit(solution)/shard_map/ppermute | solution.py:469
  128.6 2.6 %collective-permute-done.1 = f32[64,256]{1,0:T(8,128)S(1)} collective-permute-done((f32[64,256]{1,0:T(8,128)S(1)}, f32[64,256]{1,0:T(8,128)S(1)}, u32[]{:S(2)}, u32[]{:S(2)}) %collective-permute-start.1) | collective-permute-done | bytes 65568 | tf_op jit(solution)/shard_map/ppermute | solution.py:469
  131.2 5.8 %collective-permute-start.2 = (f32[64,256]{1,0:T(8,128)S(1)}, f32[64,256]{1,0:T(8,128)S(1)}, u32[]{:S(2)}, u32[]{:S(2)}) collective-permute-start(f32[64,256]{1,0:T(8,128)S(1)} %add.22), channel_id=1, source_target_pairs={{0,4},{1,5},{2,6},{3,7},{4,0},{5,1},{6,2},{7,3},{8,12},{9,13},{10,... | collective-permute-start | bytes 196616 | tf_op jit(solution)/shard_map/ppermute | solution.py:469
  137.0 2.2 %collective-permute-done.2 = f32[64,256]{1,0:T(8,128)S(1)} collective-permute-done((f32[64,256]{1,0:T(8,128)S(1)}, f32[64,256]{1,0:T(8,128)S(1)}, u32[]{:S(2)}, u32[]{:S(2)}) %collective-permute-start.2) | collective-permute-done | bytes 65568 | tf_op jit(solution)/shard_map/ppermute | solution.py:469
  139.3 3.6 %collective-permute-start.3 = (f32[64,256]{1,0:T(8,128)S(1)}, f32[64,256]{1,0:T(8,128)S(1)}, u32[]{:S(2)}, u32[]{:S(2)}) collective-permute-start(f32[64,256]{1,0:T(8,128)S(1)} %add.23), channel_id=1, source_target_pairs={{0,8},{1,9},{2,10},{3,11},{4,12},{5,13},{6,14},{7,15},{8,0},{9,1},... | collective-permute-start | bytes 196616 | tf_op jit(solution)/shard_map/ppermute | solution.py:469
  142.9 2.2 %collective-permute-done.3 = f32[64,256]{1,0:T(8,128)S(1)} collective-permute-done((f32[64,256]{1,0:T(8,128)S(1)}, f32[64,256]{1,0:T(8,128)S(1)}, u32[]{:S(2)}, u32[]{:S(2)}) %collective-permute-start.3) | collective-permute-done | bytes 65568 | tf_op jit(solution)/shard_map/ppermute | solution.py:469
  145.1 0.1 collective-permute-start.4
  145.2 0.2 sine_negate_fusion
  145.4 1.1 collective-permute-done.4.refs_2_
  146.5 6.3 %shard_map.81 = (f32[4,512]{1,0:T(4,128)S(1)}, f32[4,2,128,512]{3,2,1,0:T(8,128)}) custom-call(s32[1]{0:T(128)} %bitcast.refs_0_, f32[64,256]{1,0:T(8,128)S(1)} %add.24.refs_1_, f32[64,256]{1,0:T(8,128)S(1)} %collective-permute-done.4.refs_2_, f32[8,512]{1,0:T(8,128)S(1)} %get-tuple-element.27.refs_3_, f32[8,512]{1,0:T(8,128)S(1)} %get-tuple-element.26.refs_4_, ...), custom_call_target="tpu_custom_call" | custom-call | flops 33554432 | bytes 6291456 | tf_op jit(solution)/shard_map/pallas_call | solution.py:380
  152.7 0.6 dynamic-slice_bitcast_fusion
  (11 shorter events, 0.1 us)
Async XLA Ops:
  11.2 48.5 %all-to-all-start.1 = ((f32[16,64,512]{2,1,0:T(8,128)}), f32[16,64,512]{2,1,0:T(8,128)S(1)}, u32[]{:S(2)}, u32[]{:S(2)}) async-start(f32[16,64,512]{2,1,0:T(8,128)} %shard_map.77), calls=%async_computation.1 | async-start | bytes 4194304 | tf_op jit(solution)/shard_map/all_to_all | solution.py:484
  59.7 1.3 copy-start
  61.0 52.3 %all-to-all-start = ((f32[16,64,512]{2,1,0:T(8,128)}), f32[16,64,512]{2,1,0:T(8,128)S(1)}, u32[]{:S(2)}, u32[]{:S(2)}) async-start(f32[16,64,512]{2,1,0:T(8,128)} %shard_map.78), calls=%async_computation | async-start | bytes 4194304 | tf_op jit(solution)/shard_map/all_to_all | solution.py:484
  72.3 1.6 %copy-start.1 = (f32[16,64,512]{2,1,0:T(8,128)S(1)}, f32[16,64,512]{2,1,0:T(8,128)}, u32[]{:S(2)}) copy-start(f32[16,64,512]{2,1,0:T(8,128)} %copy-done) | copy-start | bytes 6291460
  81.8 0.6 copy-start.3
  113.4 31.9 %copy-start.4 = (s32[8]{0:T(128)S(1)}, s32[8]{0:T(128)}, u32[]{:S(2)}) copy-start(s32[8]{0:T(128)} %param.7) | copy-start | bytes 100
  113.4 33.1 %copy-start.2 = (s32[512]{0:T(512)S(1)}, s32[512]{0:T(512)}, u32[]{:S(2)}) copy-start(s32[512]{0:T(512)} %param.9) | copy-start | bytes 6148
  123.5 1.7 %collective-permute-start = (f32[64,256]{1,0:T(8,128)S(1)}, f32[64,256]{1,0:T(8,128)S(1)}, u32[]{:S(2)}, u32[]{:S(2)}) collective-permute-start(f32[64,256]{1,0:T(8,128)S(1)} %get-tuple-element.21), channel_id=1, source_target_pairs={{0,1},{1,0},{2,3},{3,2},{4,5},{5,4},{6,7},{7,6},{8,9},{9,8},{10,11... | collective-permute-start | bytes 196616 | tf_op jit(solution)/shard_map/ppermute | solution.py:469
  125.2 6.0 %collective-permute-start.1 = (f32[64,256]{1,0:T(8,128)S(1)}, f32[64,256]{1,0:T(8,128)S(1)}, u32[]{:S(2)}, u32[]{:S(2)}) collective-permute-start(f32[64,256]{1,0:T(8,128)S(1)} %add.21), channel_id=1, source_target_pairs={{0,2},{1,3},{2,0},{3,1},{4,6},{5,7},{6,4},{7,5},{8,10},{9,11},{10,... | collective-permute-start | bytes 196616 | tf_op jit(solution)/shard_map/ppermute | solution.py:469
  131.2 8.0 %collective-permute-start.2 = (f32[64,256]{1,0:T(8,128)S(1)}, f32[64,256]{1,0:T(8,128)S(1)}, u32[]{:S(2)}, u32[]{:S(2)}) collective-permute-start(f32[64,256]{1,0:T(8,128)S(1)} %add.22), channel_id=1, source_target_pairs={{0,4},{1,5},{2,6},{3,7},{4,0},{5,1},{6,2},{7,3},{8,12},{9,13},{10,... | collective-permute-start | bytes 196616 | tf_op jit(solution)/shard_map/ppermute | solution.py:469
  139.3 5.9 %collective-permute-start.3 = (f32[64,256]{1,0:T(8,128)S(1)}, f32[64,256]{1,0:T(8,128)S(1)}, u32[]{:S(2)}, u32[]{:S(2)}) collective-permute-start(f32[64,256]{1,0:T(8,128)S(1)} %add.23), channel_id=1, source_target_pairs={{0,8},{1,9},{2,10},{3,11},{4,12},{5,13},{6,14},{7,15},{8,0},{9,1},... | collective-permute-start | bytes 196616 | tf_op jit(solution)/shard_map/ppermute | solution.py:469
  145.1 1.3 collective-permute-start.4

commit v5 on v4

--- a/solution.py
+++ b/solution.py
@@ -225,7 +225,7 @@
         for b, e in chunk:
             rows += [e * blocks + b] if b == e else [e * blocks + b, b * blocks + e]
         zero = jnp.zeros((8, gram.shape[1]), jnp.float32)
-        sums = lax.fori_loop(0, LANES // 8, body, (zero,) * len(rows))
+        sums = lax.fori_loop(0, LANES // 8, body, (zero,) * len(rows), unroll=True)
         for row, value in zip(rows, sums):
             gram[row : row + 1, :] = jnp.sum(value, axis=0, keepdims=True)
 
@@ -237,13 +237,26 @@
     (re, im), grams, (x_high, x_low, gram) = refs[:2], refs[2:-3], refs[-3:]
     step = pl.program_id(0)
 
+    def put(got):
+        re[...] = got[:, :LANES]
+        im[...] = got[:, LANES:]
+
     @pl.when(step == 0)
     def _():
-        x_high[...], x_low[...] = two_terms(x[...].T)
-
-    got = dot(x_high[...], high[...]) + dot(x_low[...], high[...]) + dot(x_high[...], low[...])
-    re[...] = got[:, :LANES]
-    im[...] = got[:, LANES:]
+        depth = 2 * LANES
+        got = None
+        for at in range(0, x.shape[0], depth):
+            spot = (slice(None), slice(at, at + depth))
+            x_high[spot], x_low[spot] = terms = two_terms(x[at : at + depth, :].T)
+            w = (high[at : at + depth, :], low[at : at + depth, :])
+            part = dot(terms[0], w[0]) + dot(terms[1], w[0]) + dot(terms[0], w[1])
+            got = part if at == 0 else got + part
+        put(got)
+
+    @pl.when(step > 0)
+    def _():
+        put(dot(x_high[...], high[...]) + dot(x_low[...], high[...]) + dot(x_high[...], low[...]))
+
     gram[...] = before[...] if others else jnp.zeros_like(gram)
     gram_tile(parts + [(re, im)], blocks, gram)
     if final:
@@ -267,7 +280,7 @@
     held = pl.BlockSpec((width, LANES), lambda i, c: (0, i))
     shape = pltpu.HBM((width, bins), jnp.float32)
     flat = [a for part in others for a in part] + ([before] if others else [])
-    in_specs = [pl.BlockSpec((frames, width), lambda i, c: (0, 0))]
+    in_specs = [pl.BlockSpec(memory_space=pltpu.VMEM)]
     in_specs += [pl.BlockSpec((frames, 2 * LANES), lambda i, c: (0, i))] * 2
     in_specs += [pl.BlockSpec((a.shape[0], LANES), lambda i, c: (0, i)) for a in flat]
     square = blocks * blocks
@@ -304,7 +317,7 @@
 
 def finish_kernel(blocks, points, parts, core, mine, other, turn_re, turn_im, kept, *refs):
     spectra_refs = [(refs[2 * n], refs[2 * n + 1]) for n in range(parts)]
-    energy, modes, tiles, basis = refs[2 * parts :]
+    energy, modes, tiles, basis, levels = refs[2 * parts :]
     step = pl.program_id(0)
 
     @pl.when(step == 0)
@@ -346,7 +359,7 @@
                 ys.append((re, im))
         for m, (q, y) in enumerate(zip(done, ys)):
             level = row_dot(q, y)[0]
-            energy[m : m + 1, :] = level
+            levels[m : m + 1, :] = level
             factor = jnp.where(kept[...] > m, 1.0, 0.0) / jnp.sqrt(level)
             re, im = cmul(ph, q)
             re, im = re * factor, im * factor
@@ -354,6 +367,10 @@
                 lane = slice(t * LANES, (t + 1) * LANES)
                 basis[t, 2 * m * blocks : (2 * m + 1) * blocks, :] = re[:, lane]
                 basis[t, (2 * m + 1) * blocks : (2 * m + 2) * blocks, :] = im[:, lane]
+        owned = energy.shape[1]
+        bins = levels.shape[1]
+        turned = pltpu.roll(levels[...], (bins - core[1] * owned) % bins, 1)
+        energy[...] = turned[:MODES, :owned]
 
     where = []
     for re, im in spectra_refs:
@@ -370,7 +387,7 @@
         modes[m, 1] = total_im
 
 
-def finish(blocks, points, core, mine, other, turn, kept, parts):
+def finish(blocks, points, owned, core, mine, other, turn, kept, parts):
     square, half = mine.shape
     bins = 2 * half
     flat = [a for part in parts for a in part]
@@ -385,16 +402,17 @@
             in_specs=[whole(a) for a in small]
             + [pl.BlockSpec((a.shape[0], LANES), lambda i, c: (0, i)) for a in flat],
             out_specs=[
-                pl.BlockSpec((MODES, bins), lambda i, c: (0, 0)),
+                pl.BlockSpec((MODES, owned), lambda i, c: (0, 0)),
                 pl.BlockSpec((MODES, 2, LANES, LANES), lambda i, c: (0, 0, 0, i)),
             ],
             scratch_shapes=[
                 pltpu.VMEM((bins // LANES, square, LANES), jnp.float32),
                 pltpu.VMEM((bins // LANES, 2 * MODES * blocks, LANES), jnp.float32),
+                pltpu.VMEM((8, bins), jnp.float32),
             ],
         ),
         out_shape=[
-            jax.ShapeDtypeStruct((MODES, bins), jnp.float32),
+            jax.ShapeDtypeStruct((MODES, owned), jnp.float32),
             jax.ShapeDtypeStruct((MODES, 2, LANES, bins), jnp.float32),
         ],
         compiler_params=SMALL,
@@ -458,10 +476,11 @@
         re = jnp.sum(u[0] * q[0][:, None] - u[1] * q[1][:, None], axis=0)
         im = jnp.sum(u[0] * q[1][:, None] + u[1] * q[0][:, None], axis=0)
         modes.append(jnp.stack([re, im]))
-    return energy, jnp.stack(modes)
-
-
-CHUNKS = (4, 4)
+    held = lax.dynamic_slice_in_dim(energy, rank * (bins // ranks), bins // ranks, axis=1)
+    return held, jnp.stack(modes)
+
+
+CHUNKS = (2, 6)
 
 
 def swap_with(values, step):
@@ -495,21 +514,21 @@
         mine = mine + swap_with(mine, step)
         step *= 2
     other = swap_with(mine, 1)
-    energy, modes = finish(blocks, points, core, mine, other, turn, modes_kept, parts)
+    energy, modes = finish(
+        blocks, points, bins // ranks, jnp.stack([rank & 1, rank]), mine, other, turn, modes_kept, parts
+    )
     return energy, modes
 
 
 def local(signal, offsets, pairing, modes_kept):
     rows, blocks, points = signal.shape
     ranks = lax.axis_size("freq")
-    rank = lax.axis_index("freq")
     bins = rows * ranks // 2
     fits = points == ranks * LANES and rows % 16 == 0 and ranks >= GROUP and ranks & (ranks - 1) == 0
     fits = fits and bins % (2 * LANES) == 0 and blocks == sum(CHUNKS) == 8
     energy, modes = (tiled if fits else plain)(signal, offsets, pairing, modes_kept)
     modes = modes.reshape(MODES, 2, 2, points // ranks // 2, bins)
-    held = lax.dynamic_slice_in_dim(energy, rank * (bins // ranks), bins // ranks, axis=1)
-    return held.T, modes.transpose(4, 0, 1, 2, 3)
+    return energy.T, modes.transpose(4, 0, 1, 2, 3)
 
 
 def solution(mesh):

time: 154 us -> 150 us (0.974)
    all_to_all x2, starting transfers between devices: 18.6 us -> 14.2 us  [tiled(): lax.all_to_all(part, 'freq', split_axis=0, concat_axis=0, tiled=True)]
    ppermute x5, starting transfers between devices: 13.7 us -> 17.9 us  [swap_with(): return lax.ppermute(values, 'freq', [(i, i ^ step) for i in range(ranks)])]
    pallas_call x2, Pallas kernels: 18.1 us -> 15.9 us  [spectra(): pl.pallas_call(lambda *refs: spectra_kernel(blocks, len(others), final, *...]
  transfers between devices with their start and end apart: 7 -> 7, of which waited for: 7 -> 7; matrix products, arithmetic and copies ran while one was open for 0% -> 0% of each run, Pallas kernels for 12% -> 13%
where the time goes in v5:
time: 150 us
  waiting for transfers between devices  69.8 us (47%)
  Pallas kernels  44 us (29%)
  starting transfers between devices  32.1 us (21%)
  local copies, waits for them, and re-layouts  2.85 us (2%)
    all_to_all x2, waiting for transfers between devices, tiled(): lax.all_to_all(part, 'freq', split_axis=0, concat_axis=0, tiled=True)  60.8 us
    pallas_call x2, Pallas kernels, pack(): pl.pallas_call(lambda *refs: pack_kernel(blocks, first, count, strips, *r...  21.2 us
    ppermute x5, starting transfers between devices, swap_with(): return lax.ppermute(values, 'freq', [(i, i ^ step) for i in range(ranks)])  17.9 us
    pallas_call x2, Pallas kernels, spectra(): pl.pallas_call(lambda *refs: spectra_kernel(blocks, len(others), final, *...  15.9 us
    all_to_all x2, starting transfers between devices, tiled(): lax.all_to_all(part, 'freq', split_axis=0, concat_axis=0, tiled=True)  14.2 us
    ppermute x5, waiting for transfers between devices, swap_with(): return lax.ppermute(values, 'freq', [(i, i ^ step) for i in range(ranks)])  9.01 us
    pallas_call x1, Pallas kernels, finish(): pl.pallas_call(lambda *refs: finish_kernel(blocks, points, len(parts), *r...  6.83 us
  transfers between devices with their start and end apart: 7, of which 7 were waited for; matrix products, arithmetic and copies ran while one was open for 0% of the time, Pallas kernels for 13%

profile of v5, /device:TPU:0, one launch (start us, length us, event | category | flops | bytes accessed | tf_op | source)
XLA Modules:
  0.0 149.8 jit_solution(6992082665168564202)
XLA Ops:
  0.6 7.0 %shard_map.77 = f32[16,64,256]{2,1,0:T(8,128)} custom-call(f32[512,2048]{1,0:T(8,128)} %bitcast.15, f32[512,2048]{1,0:T(8,128)} %bitcast.16, f32[512,2048]{1,0:T(8,128)} %bitcast.17, f32[512,2048]{1,0:T(8,128)} %bitcast.18, s32[16,128]{1,0:T(8,128)} %bitcast.23), custom_call_target="tpu_custom_call" | custom-call | flops 3221225472 | bytes 8388608 | tf_op jit(solution)/shard_map/pallas_call | solution.py:172
  7.6 7.4 %all-to-all-start.1 = ((f32[16,64,256]{2,1,0:T(8,128)}), f32[16,64,256]{2,1,0:T(8,128)S(1)}, u32[]{:S(2)}, u32[]{:S(2)}) async-start(f32[16,64,256]{2,1,0:T(8,128)} %shard_map.77), calls=%async_computation.1 | async-start | bytes 2097152 | tf_op jit(solution)/shard_map/all_to_all | solution.py:503
  14.9 14.3 %shard_map.78 = f32[16,64,768]{2,1,0:T(8,128)} custom-call(f32[512,2048]{1,0:T(8,128)} %bitcast.19, f32[512,2048]{1,0:T(8,128)} %bitcast.20, f32[512,2048]{1,0:T(8,128)} %bitcast.21, f32[512,2048]{1,0:T(8,128)} %bitcast.22, s32[16,128]{1,0:T(8,128)} %bitcast.24), custom_call_target="tpu_custom_call" | custom-call | flops 9663676416 | bytes 8388608 | tf_op jit(solution)/shard_map/pallas_call | solution.py:172
  29.2 8.6 %all-to-all-done.1 = f32[16,64,256]{2,1,0:T(8,128)S(1)} async-done(((f32[16,64,256]{2,1,0:T(8,128)}), f32[16,64,256]{2,1,0:T(8,128)S(1)}, u32[]{:S(2)}, u32[]{:S(2)}) %all-to-all-start.1) | async-done | bytes 1048608 | tf_op jit(solution)/shard_map/all_to_all | solution.py:503
  37.9 1.0 copy-done
  38.9 6.9 %all-to-all-start = ((f32[16,64,768]{2,1,0:T(8,128)}), f32[16,64,768]{2,1,0:T(8,128)S(1)}, u32[]{:S(2)}, u32[]{:S(2)}) async-start(f32[16,64,768]{2,1,0:T(8,128)} %shard_map.78), calls=%async_computation | async-start | bytes 6291456 | tf_op jit(solution)/shard_map/all_to_all | solution.py:503
  45.7 1.2 copy-done.1
  47.0 5.3 %shard_map.79 = (f32[256,512]{1,0:T(8,128)}, f32[256,512]{1,0:T(8,128)}, f32[64,512]{1,0:T(8,128)S(1)}) custom-call(s32[1]{0:T(128)} %bitcast.refs_0_, f32[1024,256]{1,0:T(8,128)S(1)} %bitcast.13, bf16[1024,1024]{1,0:T(8,128)(2,1)} %constant.27.clone.refs_2_, bf16[1024,1024]{1,0:T(8,128)(2,1)} %constant.28.clone.refs_3_), custom_call_target="tpu_custom_call" | custom-call | flops 1610612736 | bytes 12582912 | tf_op jit(solution)/shard_map/pallas_call | solution.py:293
  52.3 0.7 copy-done.3
  52.9 52.2 %all-to-all-done = f32[16,64,768]{2,1,0:T(8,128)S(1)} async-done(((f32[16,64,768]{2,1,0:T(8,128)}), f32[16,64,768]{2,1,0:T(8,128)S(1)}, u32[]{:S(2)}, u32[]{:S(2)}) %all-to-all-start) | async-done | bytes 3145760 | tf_op jit(solution)/shard_map/all_to_all | solution.py:503
  105.1 10.6 %shard_map.80 = (f32[768,512]{1,0:T(8,128)}, f32[768,512]{1,0:T(8,128)}, f32[64,256]{1,0:T(8,128)S(1)}, f32[64,256]{1,0:T(8,128)S(1)}) custom-call(s32[1]{0:T(128)} %bitcast.refs_0_, f32[1024,768]{1,0:T(8,128)S(1)} %bitcast.12, bf16[1024,1024]{1,0:T(8,128)(2,1)} %constant.27.clone.refs_2_, bf16[1024,1024]{1,0:T(8,128)(2,1)} %constant.28.clone.refs_3_, ...), custom_call_target="tpu_custom_call" | custom-call | flops 4831838208 | bytes 12582912 | tf_op jit(solution)/shard_map/pallas_call | solution.py:293
  115.7 0.8 collective-permute-start
  116.5 0.9 collective-permute-done
  117.4 4.8 %collective-permute-start.1 = (f32[64,256]{1,0:T(8,128)S(1)}, f32[64,256]{1,0:T(8,128)S(1)}, u32[]{:S(2)}, u32[]{:S(2)}) collective-permute-start(f32[64,256]{1,0:T(8,128)S(1)} %add.18), channel_id=1, source_target_pairs={{0,2},{1,3},{2,0},{3,1},{4,6},{5,7},{6,4},{7,5},{8,10},{9,11},{10,... | collective-permute-start | bytes 196616 | tf_op jit(solution)/shard_map/ppermute | solution.py:488
  122.3 2.6 %collective-permute-done.1 = f32[64,256]{1,0:T(8,128)S(1)} collective-permute-done((f32[64,256]{1,0:T(8,128)S(1)}, f32[64,256]{1,0:T(8,128)S(1)}, u32[]{:S(2)}, u32[]{:S(2)}) %collective-permute-start.1) | collective-permute-done | bytes 65568 | tf_op jit(solution)/shard_map/ppermute | solution.py:488
  124.9 8.6 %collective-permute-start.2 = (f32[64,256]{1,0:T(8,128)S(1)}, f32[64,256]{1,0:T(8,128)S(1)}, u32[]{:S(2)}, u32[]{:S(2)}) collective-permute-start(f32[64,256]{1,0:T(8,128)S(1)} %add.19), channel_id=1, source_target_pairs={{0,4},{1,5},{2,6},{3,7},{4,0},{5,1},{6,2},{7,3},{8,12},{9,13},{10,... | collective-permute-start | bytes 196616 | tf_op jit(solution)/shard_map/ppermute | solution.py:488
  133.5 2.2 %collective-permute-done.2 = f32[64,256]{1,0:T(8,128)S(1)} collective-permute-done((f32[64,256]{1,0:T(8,128)S(1)}, f32[64,256]{1,0:T(8,128)S(1)}, u32[]{:S(2)}, u32[]{:S(2)}) %collective-permute-start.2) | collective-permute-done | bytes 65568 | tf_op jit(solution)/shard_map/ppermute | solution.py:488
  135.7 3.6 %collective-permute-start.3 = (f32[64,256]{1,0:T(8,128)S(1)}, f32[64,256]{1,0:T(8,128)S(1)}, u32[]{:S(2)}, u32[]{:S(2)}) collective-permute-start(f32[64,256]{1,0:T(8,128)S(1)} %add.20), channel_id=1, source_target_pairs={{0,8},{1,9},{2,10},{3,11},{4,12},{5,13},{6,14},{7,15},{8,0},{9,1},... | collective-permute-start | bytes 196616 | tf_op jit(solution)/shard_map/ppermute | solution.py:488
  139.3 0.2 sine_negate_fusion
  139.5 2.1 %collective-permute-done.3 = f32[64,256]{1,0:T(8,128)S(1)} collective-permute-done((f32[64,256]{1,0:T(8,128)S(1)}, f32[64,256]{1,0:T(8,128)S(1)}, u32[]{:S(2)}, u32[]{:S(2)}) %collective-permute-start.3) | collective-permute-done | bytes 65568 | tf_op jit(solution)/shard_map/ppermute | solution.py:488
  141.6 0.1 collective-permute-start.4
  141.7 0.1 pad_add_fusion.refs_0_
  141.8 1.2 collective-permute-done.4.refs_2_
  142.9 6.8 %shard_map.81 = (f32[4,32]{1,0:T(4,128)}, f32[4,2,128,512]{3,2,1,0:T(8,128)}) custom-call(s32[2]{0:T(128)S(1)} %pad_add_fusion.refs_0_, f32[64,256]{1,0:T(8,128)S(1)} %add.21.refs_1_, f32[64,256]{1,0:T(8,128)S(1)} %collective-permute-done.4.refs_2_, f32[8,512]{1,0:T(8,128)S(1)} %get-tuple-element.27.refs_3_, f32[8,512]{1,0:T(8,128)S(1)} %get-tuple-element.26.refs_4_, ...), custom_call_target="tpu_custom_call" | custom-call | flops 33554432 | bytes 6291456 | tf_op jit(solution)/shard_map/pallas_call | solution.py:397
  (11 shorter events, 0.1 us)
Async XLA Ops:
  7.6 30.3 %all-to-all-start.1 = ((f32[16,64,256]{2,1,0:T(8,128)}), f32[16,64,256]{2,1,0:T(8,128)S(1)}, u32[]{:S(2)}, u32[]{:S(2)}) async-start(f32[16,64,256]{2,1,0:T(8,128)} %shard_map.77), calls=%async_computation.1 | async-start | bytes 2097152 | tf_op jit(solution)/shard_map/all_to_all | solution.py:503
  37.9 1.0 copy-start
  38.9 66.2 %all-to-all-start = ((f32[16,64,768]{2,1,0:T(8,128)}), f32[16,64,768]{2,1,0:T(8,128)S(1)}, u32[]{:S(2)}, u32[]{:S(2)}) async-start(f32[16,64,768]{2,1,0:T(8,128)} %shard_map.78), calls=%async_computation | async-start | bytes 6291456 | tf_op jit(solution)/shard_map/all_to_all | solution.py:503
  45.7 1.2 copy-start.1
  52.3 0.7 copy-start.3
  105.1 34.2 %copy-start.4 = (s32[8]{0:T(128)S(1)}, s32[8]{0:T(128)}, u32[]{:S(2)}) copy-start(s32[8]{0:T(128)} %param.7) | copy-start | bytes 100
  105.1 37.8 %copy-start.2 = (s32[512]{0:T(512)S(1)}, s32[512]{0:T(512)}, u32[]{:S(2)}) copy-start(s32[512]{0:T(512)} %param.9) | copy-start | bytes 6148
  115.7 1.7 %collective-permute-start = (f32[64,256]{1,0:T(8,128)S(1)}, f32[64,256]{1,0:T(8,128)S(1)}, u32[]{:S(2)}, u32[]{:S(2)}) collective-permute-start(f32[64,256]{1,0:T(8,128)S(1)} %get-tuple-element.21), channel_id=1, source_target_pairs={{0,1},{1,0},{2,3},{3,2},{4,5},{5,4},{6,7},{7,6},{8,9},{9,8},{10,11... | collective-permute-start | bytes 196616 | tf_op jit(solution)/shard_map/ppermute | solution.py:488
  117.4 7.4 %collective-permute-start.1 = (f32[64,256]{1,0:T(8,128)S(1)}, f32[64,256]{1,0:T(8,128)S(1)}, u32[]{:S(2)}, u32[]{:S(2)}) collective-permute-start(f32[64,256]{1,0:T(8,128)S(1)} %add.18), channel_id=1, source_target_pairs={{0,2},{1,3},{2,0},{3,1},{4,6},{5,7},{6,4},{7,5},{8,10},{9,11},{10,... | collective-permute-start | bytes 196616 | tf_op jit(solution)/shard_map/ppermute | solution.py:488
  124.9 10.8 %collective-permute-start.2 = (f32[64,256]{1,0:T(8,128)S(1)}, f32[64,256]{1,0:T(8,128)S(1)}, u32[]{:S(2)}, u32[]{:S(2)}) collective-permute-start(f32[64,256]{1,0:T(8,128)S(1)} %add.19), channel_id=1, source_target_pairs={{0,4},{1,5},{2,6},{3,7},{4,0},{5,1},{6,2},{7,3},{8,12},{9,13},{10,... | collective-permute-start | bytes 196616 | tf_op jit(solution)/shard_map/ppermute | solution.py:488
  135.7 5.8 %collective-permute-start.3 = (f32[64,256]{1,0:T(8,128)S(1)}, f32[64,256]{1,0:T(8,128)S(1)}, u32[]{:S(2)}, u32[]{:S(2)}) collective-permute-start(f32[64,256]{1,0:T(8,128)S(1)} %add.20), channel_id=1, source_target_pairs={{0,8},{1,9},{2,10},{3,11},{4,12},{5,13},{6,14},{7,15},{8,0},{9,1},... | collective-permute-start | bytes 196616 | tf_op jit(solution)/shard_map/ppermute | solution.py:488
  141.6 1.3 collective-permute-start.4

commit v6 on v5

--- a/solution.py
+++ b/solution.py
@@ -316,12 +316,27 @@
 
 
 def finish_kernel(blocks, points, parts, core, mine, other, turn_re, turn_im, kept, *refs):
-    spectra_refs = [(refs[2 * n], refs[2 * n + 1]) for n in range(parts)]
-    energy, modes, tiles, basis, levels = refs[2 * parts :]
-    step = pl.program_id(0)
-
-    @pl.when(step == 0)
-    def _():
+    sources, refs = refs[: 2 * parts], refs[2 * parts :]
+    energy, modes, tiles, basis, levels, made, come, gone = refs[:8]
+    held = refs[8:]
+    steps = come.shape[0]
+
+    def arrivals(t):
+        lane = slice(t * LANES, (t + 1) * LANES)
+        return [
+            pltpu.make_async_copy(source.at[:, lane], place.at[t], come.at[t, n])
+            for n, (source, place) in enumerate(zip(sources, held))
+        ]
+
+    def departure(t):
+        lane = slice(t * LANES, (t + 1) * LANES)
+        return pltpu.make_async_copy(made.at[t], modes.at[:, :, :, lane], gone.at[t])
+
+    for t in range(steps):
+        for copy in arrivals(t):
+            copy.start()
+
+    def make_basis():
         swap = core[0] == 1
         half = mine.shape[1]
         count = 2 * half // LANES
@@ -372,44 +387,52 @@
         turned = pltpu.roll(levels[...], (bins - core[1] * owned) % bins, 1)
         energy[...] = turned[:MODES, :owned]
 
-    where = []
-    for re, im in spectra_refs:
-        where += [(re, im, n * LANES) for n in range(re.shape[0] // LANES)]
-    for m in range(MODES):
-        total_re, total_im = None, None
-        for b, (re, im, base) in enumerate(where):
-            u = (re[base : base + LANES, :], im[base : base + LANES, :])
-            q = [basis[step, pl.ds((2 * m + n) * blocks + b, 1), :] for n in (0, 1)]
-            part = cmul(u, q)
-            total_re = part[0] if b == 0 else total_re + part[0]
-            total_im = part[1] if b == 0 else total_im + part[1]
-        modes[m, 0] = total_re
-        modes[m, 1] = total_im
+    make_basis()
+    for t in range(steps):
+        for copy in arrivals(t):
+            copy.wait()
+        where = []
+        for n in range(parts):
+            re, im = held[2 * n].at[t], held[2 * n + 1].at[t]
+            where += [(re, im, n * LANES) for n in range(re.shape[0] // LANES)]
+        for m in range(MODES):
+            total = None
+            for b, (re, im, base) in enumerate(where):
+                u = (re[base : base + LANES, :], im[base : base + LANES, :])
+                q = [basis[t, (2 * m + n) * blocks + b : (2 * m + n) * blocks + b + 1, :] for n in (0, 1)]
+                part = cmul(u, q)
+                total = part if b == 0 else (total[0] + part[0], total[1] + part[1])
+            made[t, m, 0] = total[0]
+            made[t, m, 1] = total[1]
+        departure(t).start()
+    for t in range(steps):
+        departure(t).wait()
 
 
 def finish(blocks, points, owned, core, mine, other, turn, kept, parts):
     square, half = mine.shape
     bins = 2 * half
     flat = [a for part in parts for a in part]
-    whole = lambda a: pl.BlockSpec(a.shape, lambda i, c: (0, 0))
     kept = kept.reshape(1, bins)
     small = [mine, other, *turn, kept]
+    steps = bins // LANES
+    vmem = pl.BlockSpec(memory_space=pltpu.VMEM)
     return pl.pallas_call(
         lambda *refs: finish_kernel(blocks, points, len(parts), *refs),
         grid_spec=pltpu.PrefetchScalarGridSpec(
             num_scalar_prefetch=1,
-            grid=(bins // LANES,),
-            in_specs=[whole(a) for a in small]
-            + [pl.BlockSpec((a.shape[0], LANES), lambda i, c: (0, i)) for a in flat],
-            out_specs=[
-                pl.BlockSpec((MODES, owned), lambda i, c: (0, 0)),
-                pl.BlockSpec((MODES, 2, LANES, LANES), lambda i, c: (0, 0, 0, i)),
-            ],
+            grid=(1,),
+            in_specs=[vmem] * len(small) + [pl.BlockSpec(memory_space=pltpu.HBM)] * len(flat),
+            out_specs=[vmem, pl.BlockSpec(memory_space=pltpu.HBM)],
             scratch_shapes=[
-                pltpu.VMEM((bins // LANES, square, LANES), jnp.float32),
-                pltpu.VMEM((bins // LANES, 2 * MODES * blocks, LANES), jnp.float32),
+                pltpu.VMEM((steps, square, LANES), jnp.float32),
+                pltpu.VMEM((steps, 2 * MODES * blocks, LANES), jnp.float32),
                 pltpu.VMEM((8, bins), jnp.float32),
-            ],
+                pltpu.VMEM((steps, MODES, 2, LANES, LANES), jnp.float32),
+                pltpu.SemaphoreType.DMA((steps, len(flat))),
+                pltpu.SemaphoreType.DMA((steps,)),
+            ]
+            + [pltpu.VMEM((steps, a.shape[0], LANES), jnp.float32) for a in flat],
         ),
         out_shape=[
             jax.ShapeDtypeStruct((MODES, owned), jnp.float32),

time: 150 us -> 149 us (level)
  no operation moved by 1% of the time
where the time goes in v6:
time: 149 us
  waiting for transfers between devices  69.8 us (47%)
  Pallas kernels  42.7 us (29%)
  starting transfers between devices  32.1 us (22%)
  local copies, waits for them, and re-layouts  2.85 us (2%)
    all_to_all x2, waiting for transfers between devices, tiled(): lax.all_to_all(part, 'freq', split_axis=0, concat_axis=0, tiled=True)  60.8 us
    pallas_call x2, Pallas kernels, pack(): pl.pallas_call(lambda *refs: pack_kernel(blocks, first, count, strips, *r...  21.3 us
    ppermute x5, starting transfers between devices, swap_with(): return lax.ppermute(values, 'freq', [(i, i ^ step) for i in range(ranks)])  17.9 us
    pallas_call x2, Pallas kernels, spectra(): pl.pallas_call(lambda *refs: spectra_kernel(blocks, len(others), final, *...  15.9 us
    all_to_all x2, starting transfers between devices, tiled(): lax.all_to_all(part, 'freq', split_axis=0, concat_axis=0, tiled=True)  14.2 us
    ppermute x5, waiting for transfers between devices, swap_with(): return lax.ppermute(values, 'freq', [(i, i ^ step) for i in range(ranks)])  9.01 us
    pallas_call x1, Pallas kernels, finish(): pl.pallas_call(lambda *refs: finish_kernel(blocks, points, len(parts), *r...  5.51 us
  transfers between devices with their start and end apart: 7, of which 7 were waited for; matrix products, arithmetic and copies ran while one was open for 0% of the time, Pallas kernels for 13%

profile of v6, /device:TPU:0, one launch (start us, length us, event | category | flops | bytes accessed | tf_op | source)
XLA Modules:
  0.0 148.6 jit_solution(13815495417260172996)
XLA Ops:
  0.6 7.0 %shard_map.77 = f32[16,64,256]{2,1,0:T(8,128)} custom-call(f32[512,2048]{1,0:T(8,128)} %bitcast.15, f32[512,2048]{1,0:T(8,128)} %bitcast.16, f32[512,2048]{1,0:T(8,128)} %bitcast.17, f32[512,2048]{1,0:T(8,128)} %bitcast.18, s32[16,128]{1,0:T(8,128)} %bitcast.23), custom_call_target="tpu_custom_call" | custom-call | flops 3221225472 | bytes 8388608 | tf_op jit(solution)/shard_map/pallas_call | solution.py:172
  7.6 7.4 %all-to-all-start.1 = ((f32[16,64,256]{2,1,0:T(8,128)}), f32[16,64,256]{2,1,0:T(8,128)S(1)}, u32[]{:S(2)}, u32[]{:S(2)}) async-start(f32[16,64,256]{2,1,0:T(8,128)} %shard_map.77), calls=%async_computation.1 | async-start | bytes 2097152 | tf_op jit(solution)/shard_map/all_to_all | solution.py:526
  14.9 14.3 %shard_map.78 = f32[16,64,768]{2,1,0:T(8,128)} custom-call(f32[512,2048]{1,0:T(8,128)} %bitcast.19, f32[512,2048]{1,0:T(8,128)} %bitcast.20, f32[512,2048]{1,0:T(8,128)} %bitcast.21, f32[512,2048]{1,0:T(8,128)} %bitcast.22, s32[16,128]{1,0:T(8,128)} %bitcast.24), custom_call_target="tpu_custom_call" | custom-call | flops 9663676416 | bytes 8388608 | tf_op jit(solution)/shard_map/pallas_call | solution.py:172
  29.3 8.6 %all-to-all-done.1 = f32[16,64,256]{2,1,0:T(8,128)S(1)} async-done(((f32[16,64,256]{2,1,0:T(8,128)}), f32[16,64,256]{2,1,0:T(8,128)S(1)}, u32[]{:S(2)}, u32[]{:S(2)}) %all-to-all-start.1) | async-done | bytes 1048608 | tf_op jit(solution)/shard_map/all_to_all | solution.py:526
  37.9 1.0 copy-done
  38.9 6.9 %all-to-all-start = ((f32[16,64,768]{2,1,0:T(8,128)}), f32[16,64,768]{2,1,0:T(8,128)S(1)}, u32[]{:S(2)}, u32[]{:S(2)}) async-start(f32[16,64,768]{2,1,0:T(8,128)} %shard_map.78), calls=%async_computation | async-start | bytes 6291456 | tf_op jit(solution)/shard_map/all_to_all | solution.py:526
  45.8 1.2 copy-done.1
  47.0 5.3 %shard_map.79 = (f32[256,512]{1,0:T(8,128)}, f32[256,512]{1,0:T(8,128)}, f32[64,512]{1,0:T(8,128)S(1)}) custom-call(s32[1]{0:T(128)} %bitcast.refs_0_, f32[1024,256]{1,0:T(8,128)S(1)} %bitcast.13, bf16[1024,1024]{1,0:T(8,128)(2,1)} %constant.27.clone.refs_2_, bf16[1024,1024]{1,0:T(8,128)(2,1)} %constant.28.clone.refs_3_), custom_call_target="tpu_custom_call" | custom-call | flops 1610612736 | bytes 12582912 | tf_op jit(solution)/shard_map/pallas_call | solution.py:293
  52.3 0.7 copy-done.3
  52.9 52.2 %all-to-all-done = f32[16,64,768]{2,1,0:T(8,128)S(1)} async-done(((f32[16,64,768]{2,1,0:T(8,128)}), f32[16,64,768]{2,1,0:T(8,128)S(1)}, u32[]{:S(2)}, u32[]{:S(2)}) %all-to-all-start) | async-done | bytes 3145760 | tf_op jit(solution)/shard_map/all_to_all | solution.py:526
  105.1 10.6 %shard_map.80 = (f32[768,512]{1,0:T(8,128)}, f32[768,512]{1,0:T(8,128)}, f32[64,256]{1,0:T(8,128)S(1)}, f32[64,256]{1,0:T(8,128)S(1)}) custom-call(s32[1]{0:T(128)} %bitcast.refs_0_, f32[1024,768]{1,0:T(8,128)S(1)} %bitcast.12, bf16[1024,1024]{1,0:T(8,128)(2,1)} %constant.27.clone.refs_2_, bf16[1024,1024]{1,0:T(8,128)(2,1)} %constant.28.clone.refs_3_, ...), custom_call_target="tpu_custom_call" | custom-call | flops 4831838208 | bytes 12582912 | tf_op jit(solution)/shard_map/pallas_call | solution.py:293
  115.7 0.8 collective-permute-start
  116.5 0.9 collective-permute-done
  117.4 4.8 %collective-permute-start.1 = (f32[64,256]{1,0:T(8,128)S(1)}, f32[64,256]{1,0:T(8,128)S(1)}, u32[]{:S(2)}, u32[]{:S(2)}) collective-permute-start(f32[64,256]{1,0:T(8,128)S(1)} %add.18), channel_id=1, source_target_pairs={{0,2},{1,3},{2,0},{3,1},{4,6},{5,7},{6,4},{7,5},{8,10},{9,11},{10,... | collective-permute-start | bytes 196616 | tf_op jit(solution)/shard_map/ppermute | solution.py:511
  122.3 2.6 %collective-permute-done.1 = f32[64,256]{1,0:T(8,128)S(1)} collective-permute-done((f32[64,256]{1,0:T(8,128)S(1)}, f32[64,256]{1,0:T(8,128)S(1)}, u32[]{:S(2)}, u32[]{:S(2)}) %collective-permute-start.1) | collective-permute-done | bytes 65568 | tf_op jit(solution)/shard_map/ppermute | solution.py:511
  124.9 8.6 %collective-permute-start.2 = (f32[64,256]{1,0:T(8,128)S(1)}, f32[64,256]{1,0:T(8,128)S(1)}, u32[]{:S(2)}, u32[]{:S(2)}) collective-permute-start(f32[64,256]{1,0:T(8,128)S(1)} %add.19), channel_id=1, source_target_pairs={{0,4},{1,5},{2,6},{3,7},{4,0},{5,1},{6,2},{7,3},{8,12},{9,13},{10,... | collective-permute-start | bytes 196616 | tf_op jit(solution)/shard_map/ppermute | solution.py:511
  133.5 2.2 %collective-permute-done.2 = f32[64,256]{1,0:T(8,128)S(1)} collective-permute-done((f32[64,256]{1,0:T(8,128)S(1)}, f32[64,256]{1,0:T(8,128)S(1)}, u32[]{:S(2)}, u32[]{:S(2)}) %collective-permute-start.2) | collective-permute-done | bytes 65568 | tf_op jit(solution)/shard_map/ppermute | solution.py:511
  135.7 3.6 %collective-permute-start.3 = (f32[64,256]{1,0:T(8,128)S(1)}, f32[64,256]{1,0:T(8,128)S(1)}, u32[]{:S(2)}, u32[]{:S(2)}) collective-permute-start(f32[64,256]{1,0:T(8,128)S(1)} %add.20), channel_id=1, source_target_pairs={{0,8},{1,9},{2,10},{3,11},{4,12},{5,13},{6,14},{7,15},{8,0},{9,1},... | collective-permute-start | bytes 196616 | tf_op jit(solution)/shard_map/ppermute | solution.py:511
  139.3 0.2 sine_negate_fusion
  139.5 2.1 %collective-permute-done.3 = f32[64,256]{1,0:T(8,128)S(1)} collective-permute-done((f32[64,256]{1,0:T(8,128)S(1)}, f32[64,256]{1,0:T(8,128)S(1)}, u32[]{:S(2)}, u32[]{:S(2)}) %collective-permute-start.3) | collective-permute-done | bytes 65568 | tf_op jit(solution)/shard_map/ppermute | solution.py:511
  141.6 0.1 collective-permute-start.4
  141.7 0.1 pad_add_fusion.refs_0_
  141.8 1.2 collective-permute-done.4.refs_2_
  142.9 5.5 %shard_map.81 = (f32[4,32]{1,0:T(4,128)}, f32[4,2,128,512]{3,2,1,0:T(8,128)}) custom-call(s32[2]{0:T(128)S(1)} %pad_add_fusion.refs_0_, f32[64,256]{1,0:T(8,128)S(1)} %add.21.refs_1_, f32[64,256]{1,0:T(8,128)S(1)} %collective-permute-done.4.refs_2_, f32[8,512]{1,0:T(8,128)S(1)} %get-tuple-element.27.refs_3_, f32[8,512]{1,0:T(8,128)S(1)} %get-tuple-element.26.refs_4_, ...), custom_call_target="tpu_custom_call" | custom-call | flops 33554432 | bytes 6291456 | tf_op jit(solution)/shard_map/pallas_call | solution.py:420
  (11 shorter events, 0.1 us)
Async XLA Ops:
  7.6 30.3 %all-to-all-start.1 = ((f32[16,64,256]{2,1,0:T(8,128)}), f32[16,64,256]{2,1,0:T(8,128)S(1)}, u32[]{:S(2)}, u32[]{:S(2)}) async-start(f32[16,64,256]{2,1,0:T(8,128)} %shard_map.77), calls=%async_computation.1 | async-start | bytes 2097152 | tf_op jit(solution)/shard_map/all_to_all | solution.py:526
  37.9 1.0 copy-start
  38.9 66.2 %all-to-all-start = ((f32[16,64,768]{2,1,0:T(8,128)}), f32[16,64,768]{2,1,0:T(8,128)S(1)}, u32[]{:S(2)}, u32[]{:S(2)}) async-start(f32[16,64,768]{2,1,0:T(8,128)} %shard_map.78), calls=%async_computation | async-start | bytes 6291456 | tf_op jit(solution)/shard_map/all_to_all | solution.py:526
  45.7 1.2 copy-start.1
  52.3 0.7 copy-start.3
  105.1 34.3 %copy-start.4 = (s32[8]{0:T(128)S(1)}, s32[8]{0:T(128)}, u32[]{:S(2)}) copy-start(s32[8]{0:T(128)} %param.7) | copy-start | bytes 100
  105.1 37.8 %copy-start.2 = (s32[512]{0:T(512)S(1)}, s32[512]{0:T(512)}, u32[]{:S(2)}) copy-start(s32[512]{0:T(512)} %param.9) | copy-start | bytes 6148
  115.7 1.7 %collective-permute-start = (f32[64,256]{1,0:T(8,128)S(1)}, f32[64,256]{1,0:T(8,128)S(1)}, u32[]{:S(2)}, u32[]{:S(2)}) collective-permute-start(f32[64,256]{1,0:T(8,128)S(1)} %get-tuple-element.21), channel_id=1, source_target_pairs={{0,1},{1,0},{2,3},{3,2},{4,5},{5,4},{6,7},{7,6},{8,9},{9,8},{10,11... | collective-permute-start | bytes 196616 | tf_op jit(solution)/shard_map/ppermute | solution.py:511
  117.4 7.4 %collective-permute-start.1 = (f32[64,256]{1,0:T(8,128)S(1)}, f32[64,256]{1,0:T(8,128)S(1)}, u32[]{:S(2)}, u32[]{:S(2)}) collective-permute-start(f32[64,256]{1,0:T(8,128)S(1)} %add.18), channel_id=1, source_target_pairs={{0,2},{1,3},{2,0},{3,1},{4,6},{5,7},{6,4},{7,5},{8,10},{9,11},{10,... | collective-permute-start | bytes 196616 | tf_op jit(solution)/shard_map/ppermute | solution.py:511
  124.9 10.8 %collective-permute-start.2 = (f32[64,256]{1,0:T(8,128)S(1)}, f32[64,256]{1,0:T(8,128)S(1)}, u32[]{:S(2)}, u32[]{:S(2)}) collective-permute-start(f32[64,256]{1,0:T(8,128)S(1)} %add.19), channel_id=1, source_target_pairs={{0,4},{1,5},{2,6},{3,7},{4,0},{5,1},{6,2},{7,3},{8,12},{9,13},{10,... | collective-permute-start | bytes 196616 | tf_op jit(solution)/shard_map/ppermute | solution.py:511
  135.7 5.9 %collective-permute-start.3 = (f32[64,256]{1,0:T(8,128)S(1)}, f32[64,256]{1,0:T(8,128)S(1)}, u32[]{:S(2)}, u32[]{:S(2)}) collective-permute-start(f32[64,256]{1,0:T(8,128)S(1)} %add.20), channel_id=1, source_target_pairs={{0,8},{1,9},{2,10},{3,11},{4,12},{5,13},{6,14},{7,15},{8,0},{9,1},... | collective-permute-start | bytes 196616 | tf_op jit(solution)/shard_map/ppermute | solution.py:511
  141.6 1.3 collective-permute-start.4

commit v7 on v6

--- a/solution.py
+++ b/solution.py
@@ -166,7 +166,7 @@
 
 def pack(signal, pairing, first, count):
     rows, blocks, points = signal.shape
-    strips = 4
+    strips = 8
     ranks = points // LANES
     shape = (ranks, rows, count * LANES)
     return pl.pallas_call(
@@ -322,14 +322,14 @@
     steps = come.shape[0]
 
     def arrivals(t):
-        lane = slice(t * LANES, (t + 1) * LANES)
+        lane = pl.ds(pl.multiple_of(t * LANES, LANES), LANES)
         return [
             pltpu.make_async_copy(source.at[:, lane], place.at[t], come.at[t, n])
             for n, (source, place) in enumerate(zip(sources, held))
         ]
 
     def departure(t):
-        lane = slice(t * LANES, (t + 1) * LANES)
+        lane = pl.ds(pl.multiple_of(t * LANES, LANES), LANES)
         return pltpu.make_async_copy(made.at[t], modes.at[:, :, :, lane], gone.at[t])
 
     for t in range(steps):
@@ -388,7 +388,8 @@
         energy[...] = turned[:MODES, :owned]
 
     make_basis()
-    for t in range(steps):
+
+    def project(t, carry):
         for copy in arrivals(t):
             copy.wait()
         where = []
@@ -399,12 +400,15 @@
             total = None
             for b, (re, im, base) in enumerate(where):
                 u = (re[base : base + LANES, :], im[base : base + LANES, :])
-                q = [basis[t, (2 * m + n) * blocks + b : (2 * m + n) * blocks + b + 1, :] for n in (0, 1)]
+                q = [basis[t, pl.ds((2 * m + n) * blocks + b, 1), :] for n in (0, 1)]
                 part = cmul(u, q)
                 total = part if b == 0 else (total[0] + part[0], total[1] + part[1])
             made[t, m, 0] = total[0]
             made[t, m, 1] = total[1]
         departure(t).start()
+        return carry
+
+    lax.fori_loop(0, steps, project, 0)
     for t in range(steps):
         departure(t).wait()
 

time: 149 us -> 149 us (level)
  no operation moved by 1% of the time
where the time goes in v7:
time: 149 us; the launch traced here: 148 us
  waiting for transfers between devices  69.9 us (47%)
  Pallas kernels  42.5 us (29%)
  starting transfers between devices  32.1 us (22%)
  local copies, waits for them, and re-layouts  2.85 us (2%)
    all_to_all x2, waiting for transfers between devices, tiled(): lax.all_to_all(part, 'freq', split_axis=0, concat_axis=0, tiled=True)  60.8 us
    pallas_call x2, Pallas kernels, pack(): pl.pallas_call(lambda *refs: pack_kernel(blocks, first, count, strips, *r...  21.1 us
    ppermute x5, starting transfers between devices, swap_with(): return lax.ppermute(values, 'freq', [(i, i ^ step) for i in range(ranks)])  17.9 us
    pallas_call x2, Pallas kernels, spectra(): pl.pallas_call(lambda *refs: spectra_kernel(blocks, len(others), final, *...  15.9 us
    all_to_all x2, starting transfers between devices, tiled(): lax.all_to_all(part, 'freq', split_axis=0, concat_axis=0, tiled=True)  14.2 us
    ppermute x5, waiting for transfers between devices, swap_with(): return lax.ppermute(values, 'freq', [(i, i ^ step) for i in range(ranks)])  9.01 us
    pallas_call x1, Pallas kernels, finish(): pl.pallas_call(lambda *refs: finish_kernel(blocks, points, len(parts), *r...  5.51 us
  transfers between devices with their start and end apart: 7, of which 7 were waited for; matrix products, arithmetic and copies ran while one was open for 0% of the time, Pallas kernels for 13%

profile of v7, /device:TPU:0, one launch (start us, length us, event | category | flops | bytes accessed | tf_op | source)
XLA Modules:
  0.0 148.5 jit_solution(5396954501585216485)
XLA Ops:
  0.6 6.8 %shard_map.77 = f32[16,64,256]{2,1,0:T(8,128)} custom-call(f32[512,2048]{1,0:T(8,128)} %bitcast.15, f32[512,2048]{1,0:T(8,128)} %bitcast.16, f32[512,2048]{1,0:T(8,128)} %bitcast.17, f32[512,2048]{1,0:T(8,128)} %bitcast.18, f32[512,2048]{1,0:T(8,128)} %bitcast.19, f32[512,2048]{1,0:T(8,128)} %bitcast.20, f32[512,2048]{1,0:T(8,128)} %bitcast.21, ...), custom_call_target="tpu_custom_call" | custom-call | flops 3221225472 | bytes 8388608 | tf_op jit(solution)/shard_map/pallas_call | solution.py:172
  7.5 7.4 %all-to-all-start.1 = ((f32[16,64,256]{2,1,0:T(8,128)}), f32[16,64,256]{2,1,0:T(8,128)S(1)}, u32[]{:S(2)}, u32[]{:S(2)}) async-start(f32[16,64,256]{2,1,0:T(8,128)} %shard_map.77), calls=%async_computation.1 | async-start | bytes 2097152 | tf_op jit(solution)/shard_map/all_to_all | solution.py:530
  14.8 14.3 %shard_map.78 = f32[16,64,768]{2,1,0:T(8,128)} custom-call(f32[512,2048]{1,0:T(8,128)} %bitcast.23, f32[512,2048]{1,0:T(8,128)} %bitcast.24, f32[512,2048]{1,0:T(8,128)} %bitcast.25, f32[512,2048]{1,0:T(8,128)} %bitcast.26, f32[512,2048]{1,0:T(8,128)} %bitcast.27, f32[512,2048]{1,0:T(8,128)} %bitcast.28, f32[512,2048]{1,0:T(8,128)} %bitcast.29, ...), custom_call_target="tpu_custom_call" | custom-call | flops 9663676416 | bytes 8388608 | tf_op jit(solution)/shard_map/pallas_call | solution.py:172
  29.1 8.7 %all-to-all-done.1 = f32[16,64,256]{2,1,0:T(8,128)S(1)} async-done(((f32[16,64,256]{2,1,0:T(8,128)}), f32[16,64,256]{2,1,0:T(8,128)S(1)}, u32[]{:S(2)}, u32[]{:S(2)}) %all-to-all-start.1) | async-done | bytes 1048608 | tf_op jit(solution)/shard_map/all_to_all | solution.py:530
  37.8 1.0 copy-done
  38.7 6.9 %all-to-all-start = ((f32[16,64,768]{2,1,0:T(8,128)}), f32[16,64,768]{2,1,0:T(8,128)S(1)}, u32[]{:S(2)}, u32[]{:S(2)}) async-start(f32[16,64,768]{2,1,0:T(8,128)} %shard_map.78), calls=%async_computation | async-start | bytes 6291456 | tf_op jit(solution)/shard_map/all_to_all | solution.py:530
  45.6 1.2 copy-done.1
  46.9 5.3 %shard_map.79 = (f32[256,512]{1,0:T(8,128)}, f32[256,512]{1,0:T(8,128)}, f32[64,512]{1,0:T(8,128)S(1)}) custom-call(s32[1]{0:T(128)} %bitcast.refs_0_, f32[1024,256]{1,0:T(8,128)S(1)} %bitcast.13, bf16[1024,1024]{1,0:T(8,128)(2,1)} %constant.27.clone.refs_2_, bf16[1024,1024]{1,0:T(8,128)(2,1)} %constant.28.clone.refs_3_), custom_call_target="tpu_custom_call" | custom-call | flops 1610612736 | bytes 12582912 | tf_op jit(solution)/shard_map/pallas_call | solution.py:293
  52.1 0.7 copy-done.3
  52.8 52.2 %all-to-all-done = f32[16,64,768]{2,1,0:T(8,128)S(1)} async-done(((f32[16,64,768]{2,1,0:T(8,128)}), f32[16,64,768]{2,1,0:T(8,128)S(1)}, u32[]{:S(2)}, u32[]{:S(2)}) %all-to-all-start) | async-done | bytes 3145760 | tf_op jit(solution)/shard_map/all_to_all | solution.py:530
  105.0 10.6 %shard_map.80 = (f32[768,512]{1,0:T(8,128)}, f32[768,512]{1,0:T(8,128)}, f32[64,256]{1,0:T(8,128)S(1)}, f32[64,256]{1,0:T(8,128)S(1)}) custom-call(s32[1]{0:T(128)} %bitcast.refs_0_, f32[1024,768]{1,0:T(8,128)S(1)} %bitcast.12, bf16[1024,1024]{1,0:T(8,128)(2,1)} %constant.27.clone.refs_2_, bf16[1024,1024]{1,0:T(8,128)(2,1)} %constant.28.clone.refs_3_, ...), custom_call_target="tpu_custom_call" | custom-call | flops 4831838208 | bytes 12582912 | tf_op jit(solution)/shard_map/pallas_call | solution.py:293
  115.6 0.8 collective-permute-start
  116.4 0.9 collective-permute-done
  117.3 4.8 %collective-permute-start.1 = (f32[64,256]{1,0:T(8,128)S(1)}, f32[64,256]{1,0:T(8,128)S(1)}, u32[]{:S(2)}, u32[]{:S(2)}) collective-permute-start(f32[64,256]{1,0:T(8,128)S(1)} %add.18), channel_id=1, source_target_pairs={{0,2},{1,3},{2,0},{3,1},{4,6},{5,7},{6,4},{7,5},{8,10},{9,11},{10,... | collective-permute-start | bytes 196616 | tf_op jit(solution)/shard_map/ppermute | solution.py:515
  122.1 2.6 %collective-permute-done.1 = f32[64,256]{1,0:T(8,128)S(1)} collective-permute-done((f32[64,256]{1,0:T(8,128)S(1)}, f32[64,256]{1,0:T(8,128)S(1)}, u32[]{:S(2)}, u32[]{:S(2)}) %collective-permute-start.1) | collective-permute-done | bytes 65568 | tf_op jit(solution)/shard_map/ppermute | solution.py:515
  124.8 8.6 %collective-permute-start.2 = (f32[64,256]{1,0:T(8,128)S(1)}, f32[64,256]{1,0:T(8,128)S(1)}, u32[]{:S(2)}, u32[]{:S(2)}) collective-permute-start(f32[64,256]{1,0:T(8,128)S(1)} %add.19), channel_id=1, source_target_pairs={{0,4},{1,5},{2,6},{3,7},{4,0},{5,1},{6,2},{7,3},{8,12},{9,13},{10,... | collective-permute-start | bytes 196616 | tf_op jit(solution)/shard_map/ppermute | solution.py:515
  133.4 2.2 %collective-permute-done.2 = f32[64,256]{1,0:T(8,128)S(1)} collective-permute-done((f32[64,256]{1,0:T(8,128)S(1)}, f32[64,256]{1,0:T(8,128)S(1)}, u32[]{:S(2)}, u32[]{:S(2)}) %collective-permute-start.2) | collective-permute-done | bytes 65568 | tf_op jit(solution)/shard_map/ppermute | solution.py:515
  135.6 3.6 %collective-permute-start.3 = (f32[64,256]{1,0:T(8,128)S(1)}, f32[64,256]{1,0:T(8,128)S(1)}, u32[]{:S(2)}, u32[]{:S(2)}) collective-permute-start(f32[64,256]{1,0:T(8,128)S(1)} %add.20), channel_id=1, source_target_pairs={{0,8},{1,9},{2,10},{3,11},{4,12},{5,13},{6,14},{7,15},{8,0},{9,1},... | collective-permute-start | bytes 196616 | tf_op jit(solution)/shard_map/ppermute | solution.py:515
  139.2 0.2 sine_negate_fusion
  139.4 2.1 %collective-permute-done.3 = f32[64,256]{1,0:T(8,128)S(1)} collective-permute-done((f32[64,256]{1,0:T(8,128)S(1)}, f32[64,256]{1,0:T(8,128)S(1)}, u32[]{:S(2)}, u32[]{:S(2)}) %collective-permute-start.3) | collective-permute-done | bytes 65568 | tf_op jit(solution)/shard_map/ppermute | solution.py:515
  141.5 0.1 collective-permute-start.4
  141.6 0.1 pad_add_fusion.refs_0_
  141.6 1.2 collective-permute-done.4.refs_2_
  142.8 5.5 %shard_map.81 = (f32[4,32]{1,0:T(4,128)}, f32[4,2,128,512]{3,2,1,0:T(8,128)}) custom-call(s32[2]{0:T(128)S(1)} %pad_add_fusion.refs_0_, f32[64,256]{1,0:T(8,128)S(1)} %add.21.refs_1_, f32[64,256]{1,0:T(8,128)S(1)} %collective-permute-done.4.refs_2_, f32[8,512]{1,0:T(8,128)S(1)} %get-tuple-element.27.refs_3_, f32[8,512]{1,0:T(8,128)S(1)} %get-tuple-element.26.refs_4_, ...), custom_call_target="tpu_custom_call" | custom-call | flops 33554432 | bytes 6291456 | tf_op jit(solution)/shard_map/pallas_call | solution.py:424
  (11 shorter events, 0.1 us)
Async XLA Ops:
  7.5 30.3 %all-to-all-start.1 = ((f32[16,64,256]{2,1,0:T(8,128)}), f32[16,64,256]{2,1,0:T(8,128)S(1)}, u32[]{:S(2)}, u32[]{:S(2)}) async-start(f32[16,64,256]{2,1,0:T(8,128)} %shard_map.77), calls=%async_computation.1 | async-start | bytes 2097152 | tf_op jit(solution)/shard_map/all_to_all | solution.py:530
  37.8 1.0 copy-start
  38.7 66.2 %all-to-all-start = ((f32[16,64,768]{2,1,0:T(8,128)}), f32[16,64,768]{2,1,0:T(8,128)S(1)}, u32[]{:S(2)}, u32[]{:S(2)}) async-start(f32[16,64,768]{2,1,0:T(8,128)} %shard_map.78), calls=%async_computation | async-start | bytes 6291456 | tf_op jit(solution)/shard_map/all_to_all | solution.py:530
  45.6 1.2 copy-start.1
  52.1 0.7 copy-start.3
  105.0 34.2 %copy-start.4 = (s32[8]{0:T(128)S(1)}, s32[8]{0:T(128)}, u32[]{:S(2)}) copy-start(s32[8]{0:T(128)} %param.7) | copy-start | bytes 100
  105.0 37.8 %copy-start.2 = (s32[512]{0:T(512)S(1)}, s32[512]{0:T(512)}, u32[]{:S(2)}) copy-start(s32[512]{0:T(512)} %param.9) | copy-start | bytes 6148
  115.6 1.7 %collective-permute-start = (f32[64,256]{1,0:T(8,128)S(1)}, f32[64,256]{1,0:T(8,128)S(1)}, u32[]{:S(2)}, u32[]{:S(2)}) collective-permute-start(f32[64,256]{1,0:T(8,128)S(1)} %get-tuple-element.21), channel_id=1, source_target_pairs={{0,1},{1,0},{2,3},{3,2},{4,5},{5,4},{6,7},{7,6},{8,9},{9,8},{10,11... | collective-permute-start | bytes 196616 | tf_op jit(solution)/shard_map/ppermute | solution.py:515
  117.3 7.4 %collective-permute-start.1 = (f32[64,256]{1,0:T(8,128)S(1)}, f32[64,256]{1,0:T(8,128)S(1)}, u32[]{:S(2)}, u32[]{:S(2)}) collective-permute-start(f32[64,256]{1,0:T(8,128)S(1)} %add.18), channel_id=1, source_target_pairs={{0,2},{1,3},{2,0},{3,1},{4,6},{5,7},{6,4},{7,5},{8,10},{9,11},{10,... | collective-permute-start | bytes 196616 | tf_op jit(solution)/shard_map/ppermute | solution.py:515
  124.8 10.8 %collective-permute-start.2 = (f32[64,256]{1,0:T(8,128)S(1)}, f32[64,256]{1,0:T(8,128)S(1)}, u32[]{:S(2)}, u32[]{:S(2)}) collective-permute-start(f32[64,256]{1,0:T(8,128)S(1)} %add.19), channel_id=1, source_target_pairs={{0,4},{1,5},{2,6},{3,7},{4,0},{5,1},{6,2},{7,3},{8,12},{9,13},{10,... | collective-permute-start | bytes 196616 | tf_op jit(solution)/shard_map/ppermute | solution.py:515
  135.6 5.9 %collective-permute-start.3 = (f32[64,256]{1,0:T(8,128)S(1)}, f32[64,256]{1,0:T(8,128)S(1)}, u32[]{:S(2)}, u32[]{:S(2)}) collective-permute-start(f32[64,256]{1,0:T(8,128)S(1)} %add.20), channel_id=1, source_target_pairs={{0,8},{1,9},{2,10},{3,11},{4,12},{5,13},{6,14},{7,15},{8,0},{9,1},... | collective-permute-start | bytes 196616 | tf_op jit(solution)/shard_map/ppermute | solution.py:515
  141.5 1.3 collective-permute-start.4
